TPU v7x, 256 devices: a whole 4x4x8 slice. The times are simulated.
256 devices in a mesh: ctx: 32 (over z, x), tp: 8 (over y, core).
Axes of the slice: x: 4, y: 4, z: 8, core: 2. Of those that a mesh axis runs over, the one named last changes fastest.
Arguments:
- queries: bfloat16 [16384, 64, 128], P('ctx', 'tp'), may hold values from -6 to 6
- key_rows: bfloat16 [16384, 8, 128], P('ctx', 'tp'), may hold values from -6 to 6
- value_rows: bfloat16 [16384, 8, 128], P('ctx', 'tp'), may hold values from -6 to 6
- segments: int32 [128], replicated, may hold values from 0 to 15, never falling along the last dimension, each value on 1 to 72 neighbouring positions
- gate_input: bfloat16 [16384, 8192], P('ctx', 'tp'), may hold values from -360 to 360
- state_proj: bfloat16 [16384, 2, 8, 128], P('ctx', None, 'tp'), may hold values from -1.5 to 1.5
- step_input: float32 [16384, 128], P('ctx', 'tp'), may hold values from -3 to 3
- step_bias: float32 [128], P('tp'), may hold values from -1 to 1
- decay_rate: float32 [128], P('tp'), may hold values from 6.1035157e-06 to 0.05
- skip_gain: float32 [128], P('tp'), may hold values from 0.5 to 1.5
- conv_input: float32 [4, 8192], P(None, 'tp'), may hold values from -3 to 3
- conv_state: float32 [4, 2, 8, 128], P(None, None, 'tp'), may hold values from -3 to 3
- norm_gain: float32 [8192], P('tp'), may hold values from 0.5 to 1.5
Outputs:
- attention_out: bfloat16 [16384, 8192], P('ctx', 'tp')
- mixer_out: bfloat16 [16384, 8192], P('ctx', 'tp')
Inputs may be any that keep to these rules, and one draw needn't show every extreme that they name: `segments`: document numbers of the blocks of 128 tokens never fall; each document spans 1 to 72 whole blocks, and one spans exactly 72.
All inputs are finite; a program needn't handle non-finite values.
Results may differ from a plain program's by a relative error of at most 0.0075.
Values may be sent and summed in bfloat16 or wider, within the bound.
A program may use at most 128 MiB of HBM per device.

v0:
```python
import math

import jax
import jax.numpy as jnp
from jax import lax
from jax.sharding import PartitionSpec as P

SSM_HEADS = 128
SSM_HEAD_DIM = 64
CONV_TAPS = 4
BLOCK = 128


full_prec = lax.Precision.HIGHEST
norm_eps = 1e-05


def from_behind(value, axis, steps):
    count = lax.axis_size(axis)
    leading, last = (max(0, -steps), min(count, count - steps))
    return lax.ppermute(value, axis, [(source, source + steps) for source in range(leading, last)])


def prefix_2(part, axis, combine, identity):
    place = lax.axis_index(axis)
    gathered = jax.tree.map(lambda a: lax.all_gather(a, axis), part)
    state = jax.tree.map(lambda a, e: jnp.zeros_like(a) + jnp.asarray(e, a.dtype), part, identity)

    def one(step, state):
        return combine(
            state, jax.tree.map(lambda a: lax.dynamic_index_in_dim(a, step, 0, False), gathered)
        )

    return lax.fori_loop(0, place, one, state)


def token_segments(segments, positions):
    block_total = segments.shape[0]
    before = jnp.concatenate([jnp.zeros((1,), jnp.int32), segments[:-1]])
    increments = segments - before
    block_starts = jnp.arange(block_total, dtype=jnp.int32) * BLOCK
    reached = (positions[:, None] >= block_starts[None, :]).astype(jnp.int32)
    return jnp.sum(reached * increments[None, :], axis=1)


def attend_block(
    carried, grouped, query_pos, query_seg, key_blk, value_blk, key_pos, segments, score_scale
):
    key_seg = token_segments(segments, key_pos)
    allowed = (
        (key_pos[None, :] >= 0)
        & (key_pos[None, :] <= query_pos[:, None])
        & (key_seg[None, :] == query_seg[:, None])
    )

    def update(running):
        run_max, run_sum, run_acc = running
        key_mask = allowed[:, None, None, :]
        scores = (
            jnp.einsum("qhgd,khd->qhgk", grouped, key_blk, preferred_element_type=jnp.float32)
            * score_scale
        )
        block_max = jnp.max(jnp.where(key_mask, scores, -1e30), axis=-1)
        new_max = jnp.maximum(run_max, block_max)
        weights = jnp.where(key_mask, jnp.exp(scores - new_max[..., None]), 0.0)
        shrink = jnp.exp(run_max - new_max)
        new_sum = run_sum * shrink + jnp.sum(weights, axis=-1)
        new_acc = run_acc * shrink[..., None] + jnp.einsum(
            "qhgk,khd->qhgd",
            weights.astype(jnp.bfloat16),
            value_blk,
            preferred_element_type=jnp.float32,
        )
        return (new_max, new_sum, new_acc)

    return lax.cond(jnp.any(allowed), update, lambda running: running, carried)


def chain_states(earlier, later):
    return (earlier[0] * later[0], later[0][:, None, None] * earlier[1] + later[1])


def local(
    queries,
    key_rows,
    value_rows,
    segments,
    gate_input,
    state_proj,
    step_input,
    step_bias,
    decay_rate,
    skip_gain,
    conv_input,
    conv_state,
    norm_gain,
):
    tok_local = queries.shape[0]
    head_local = queries.shape[1]
    head_width = queries.shape[2]
    kv_local = key_rows.shape[1]
    group_size = head_local // kv_local
    ctx_count = lax.axis_size("ctx")
    my_index = lax.axis_index("ctx")
    local_pos = my_index * tok_local + jnp.arange(tok_local, dtype=jnp.int32)
    score_scale = 1.0 / math.sqrt(head_width)
    grouped = queries.reshape(tok_local, kv_local, group_size, head_width)
    query_seg = token_segments(segments, local_pos)

    def fold_keys(carried, portion, first_row):
        key_part, value_part = portion
        rows_here = key_part.shape[0]
        key_pos = first_row + jnp.arange(rows_here, dtype=jnp.int32)
        return attend_block(
            carried,
            grouped,
            local_pos,
            query_seg,
            key_part,
            value_part,
            key_pos,
            segments,
            score_scale,
        )

    start_max = jnp.full((tok_local, kv_local, group_size), -1e30, jnp.float32)
    start_sum = jnp.zeros((tok_local, kv_local, group_size), jnp.float32)
    start_acc = jnp.zeros((tok_local, kv_local, group_size, head_width), jnp.float32)
    block_count = segments.shape[0]
    doc_tokens = (block_count // 2 + 2 * (tok_local // BLOCK)) * BLOCK
    reach = min(ctx_count - 1, (doc_tokens - 1) // tok_local + 1)
    running = fold_keys(
        (start_max, start_sum, start_acc), (key_rows, value_rows), my_index * tok_local
    )

    def walk_back(back_step, state):
        key_part, value_part, run_state = state
        key_part, value_part = from_behind((key_part, value_part), "ctx", 1)
        run_state = fold_keys(run_state, (key_part, value_part), (my_index - back_step) * tok_local)
        return (key_part, value_part, run_state)

    _, _, running = lax.fori_loop(1, reach + 1, walk_back, (key_rows, value_rows, running))
    run_max, run_sum, run_acc = running
    attended = (
        (run_acc / run_sum[..., None])
        .reshape(tok_local, head_local * head_width)
        .astype(jnp.bfloat16)
    )
    rim_rows = CONV_TAPS - 1
    prev_input, prev_state = from_behind(
        (attended[tok_local - rim_rows :], state_proj[tok_local - rim_rows :]), "ctx", 1
    )
    input_ext = jnp.concatenate([prev_input, attended])
    state_ext = jnp.concatenate([prev_state, state_proj])
    ext_pos = my_index * tok_local - rim_rows + jnp.arange(tok_local + rim_rows, dtype=jnp.int32)
    ext_seg = token_segments(segments, ext_pos)
    local_seg = ext_seg[rim_rows:]
    input_conv = jnp.zeros(attended.shape, jnp.float32)
    state_conv = jnp.zeros(state_proj.shape, jnp.float32)
    for tap_id in range(CONV_TAPS):
        offset = rim_rows - tap_id
        same_doc = (
            (ext_pos[offset : offset + tok_local] >= 0)
            & (ext_seg[offset : offset + tok_local] == local_seg)
        ).astype(jnp.float32)
        input_conv = (
            input_conv
            + conv_input[tap_id][None, :]
            * input_ext[offset : offset + tok_local].astype(jnp.float32)
            * same_doc[:, None]
        )
        state_conv = (
            state_conv
            + conv_state[tap_id][None]
            * state_ext[offset : offset + tok_local].astype(jnp.float32)
            * same_doc[:, None, None, None]
        )
    input_conv = jax.nn.silu(input_conv)
    state_conv = jax.nn.silu(state_conv)
    heads_local = step_input.shape[1]
    groups_local = state_proj.shape[2]
    state_width = state_proj.shape[3]
    per_group = heads_local // groups_local
    ssm_width = input_conv.shape[1] // heads_local
    stretches = tok_local // BLOCK
    step_dt = jax.nn.softplus(step_input + step_bias[None, :])
    log_fac = -step_dt * decay_rate[None, :]
    input_stretch = input_conv.reshape(stretches, BLOCK, heads_local, ssm_width)
    write_stretch = state_conv[:, 0].reshape(stretches, BLOCK, groups_local, state_width)
    read_stretch = state_conv[:, 1].reshape(stretches, BLOCK, groups_local, state_width)
    step_stretch = step_dt.reshape(stretches, BLOCK, heads_local)
    log_cum = jnp.cumsum(log_fac.reshape(stretches, BLOCK, heads_local), axis=1)
    causal = (jnp.arange(BLOCK)[:, None] >= jnp.arange(BLOCK)[None, :])[None, :, :, None]
    log_gap = log_cum[:, :, None, :] - log_cum[:, None, :, :]
    decay_mat = jnp.where(causal, jnp.exp(jnp.where(causal, log_gap, 0.0)), 0.0)
    intersection = jnp.einsum("cign,cjgn->cijg", read_stretch, write_stretch, precision=full_prec)
    intersection_heads = jnp.repeat(intersection, per_group, axis=3)
    mixing = intersection_heads * decay_mat * step_stretch[:, None, :, :]
    intra_out = jnp.einsum("cijh,cjhp->cihp", mixing, input_stretch, precision=full_prec)
    to_end = jnp.exp(log_cum[:, -1:, :] - log_cum) * step_stretch
    write_heads = jnp.repeat(write_stretch, per_group, axis=2)
    read_heads = jnp.repeat(read_stretch, per_group, axis=2)
    stretch_state = jnp.einsum(
        "cjh,cjhp,cjhn->chpn", to_end, input_stretch, write_heads, precision=full_prec
    )
    first_pos = my_index * tok_local + jnp.arange(stretches, dtype=jnp.int32) * BLOCK
    first_seg = token_segments(segments, first_pos)
    prior_seg = token_segments(segments, first_pos - 1)
    keep_state = jnp.where((first_pos == 0) | (first_seg != prior_seg), 0.0, 1.0).astype(
        jnp.float32
    )
    stretch_trans = keep_state[:, None] * jnp.exp(log_cum[:, -1, :])

    def walk_stretches(carried, inputs):
        running_state, product = carried
        factor_now, state_now = inputs
        return (
            (factor_now[:, None, None] * running_state + state_now, product * factor_now),
            (running_state, product),
        )

    zero_state = jnp.zeros((heads_local, ssm_width, state_width), jnp.float32)
    (local_end, total_trans), (entering, prefix) = lax.scan(
        walk_stretches,
        (zero_state, jnp.ones((heads_local,), jnp.float32)),
        (stretch_trans, stretch_state),
    )
    incoming = prefix_2(
        (total_trans, local_end), "ctx", chain_states, (jnp.ones_like(total_trans), zero_state)
    )[1]
    entering = entering + prefix[:, :, None, None] * incoming[None]
    state_out = jnp.einsum("cihn,chpn->cihp", read_heads, entering, precision=full_prec)
    state_out = state_out * (keep_state[:, None, None] * jnp.exp(log_cum))[..., None]
    scan_out = intra_out + state_out + skip_gain[None, None, :, None] * input_stretch
    gated_out = scan_out.reshape(tok_local, heads_local * ssm_width) * jax.nn.silu(
        gate_input.astype(jnp.float32)
    )
    squares = lax.psum(jnp.sum(gated_out * gated_out, axis=1), "tp")
    mean_square = squares / (SSM_HEADS * SSM_HEAD_DIM)
    mixer_out = (
        gated_out * norm_gain[None, :] * lax.rsqrt(mean_square[:, None] + norm_eps)
    ).astype(jnp.bfloat16)
    return (attended, mixer_out)


def solution(mesh):
    placed = (
        P("ctx", "tp", None),
        P("ctx", "tp", None),
        P("ctx", "tp", None),
        P(),
        P("ctx", "tp"),
        P("ctx", None, "tp", None),
        P("ctx", "tp"),
        P("tp"),
        P("tp"),
        P("tp"),
        P(None, "tp"),
        P(None, None, "tp", None),
        P("tp"),
    )
    return jax.shard_map(
        local,
        mesh=mesh,
        in_specs=placed,
        out_specs=(P("ctx", "tp"), P("ctx", "tp")),
        check_vma=False,
    )
```

profile of v0, /device:TPU:230, one launch (start us, length us, event | category | flops | bytes accessed | tf_op | source)
XLA Modules:
  0.0 675.2 jit_solution(16514621111067456359)
XLA Ops:
  15.4 7.7 %conditional.2 = (f32[512,1,8]{0,2,1:T(8,128)S(1)}, f32[512,1,8]{0,2,1:T(8,128)}, f32[512,1,8,128]{3,0,2,1:T(8,128)S(1)}) conditional(s32[]{:T(128)} %convert_element_type.74, () %tuple.55, (pred[512,512]{0,1:T(8,128)(4,1)S(1)}, bf16[512,1,128]{2,0,1:T(8,128)(2,1)}, bf16[512,1,8,128]{3,0,2,1:T(8,128)(2,1)S(1)}, bf16[512,1,128]{2,0,1:T(8,128)(2,1)}) %tuple.146), branch_computations={%region_2.0_spmd, %region_3.6_spmd} | conditional | flops 1097355264 | bytes 30081076 | solution.py:76
  15.4 2.4 fusion.2
  17.9 2.8 fusion.11
  23.1 313.5 %while.54 = (s32[]{:T(128)}, bf16[512,1,128]{2,0,1:T(8,128)(2,1)}, bf16[512,1,128]{2,0,1:T(8,128)(2,1)}, f32[512,1,8]{0,2,1:T(8,128)S(1)}, f32[512,1,8]{0,2,1:T(...) while((s32[]{:T(128)}, bf16[512,1,128]{2,0,1:T(8,128)(2,1)}, ...), condition=%wide.region_13.14_spmd.clone, body=%wide.region_6.13_spmd.clone.sunk | while | flops 1099380352 | bytes 33573736 | solution.py:142
  29.0 2.4 collective-permute-done
  33.4 8.3 %conditional.5 = ((f32[512,1,8]{0,2,1:T(8,128)S(1)}, f32[512,1,8]{0,2,1:T(8,128)}, f32[512,1,8,128]{3,0,2,1:T(8,128)S(1)})) conditional(s32[]{:T(128)} %convert_element_type.135, (f32[512,1,8]{0,2,1:T(8,128)S(1)}, f32[512,1,8]{0,2,1:T(8,128)}, f32[512,1,8,128]{3,0,2,1:T(8,128)S(1)}) %tuple.125, (pred[512,512]{0,1:T(8,128)(4,1)S(1)}, ...), branch_computations={%region_9.9_spmd, %region_10.12_spmd} | conditional | flops 1097871360 | bytes 31719456 | solution.py:76
  38.0 3.7 bitcast_add_fusion.2
  49.8 2.4 collective-permute-done
  62.0 9.5 %collective-permute-done = bf16[512,1,128]{2,0,1:T(8,128)(2,1)S(1)} collective-permute-done((bf16[512,1,128]{2,0,1:T(8,128)(2,1)}, bf16[512,1,128]{2,0,1:T(8,128)(2,1)S(1)}, u32[]{:S(2)}, u32[]{:S(2)}) %collective-permute-start) | collective-permute-done | bytes 131104 | tf_op jit(solution)/shard_map/while/body/eval_jaxpr/ppermute | solution.py:21
  93.6 2.0 collective-permute-done.1
  104.9 2.0 collective-permute-done.1
  115.0 3.0 collective-permute-done
  118.1 2.0 collective-permute-done.1
  128.2 3.3 collective-permute-done
  131.5 2.0 collective-permute-done.1
  141.6 3.3 collective-permute-done
  144.9 2.0 collective-permute-done.1
  155.0 3.3 collective-permute-done
  158.3 2.0 collective-permute-done.1
  168.5 11.4 %collective-permute-done = bf16[512,1,128]{2,0,1:T(8,128)(2,1)S(1)} collective-permute-done((bf16[512,1,128]{2,0,1:T(8,128)(2,1)}, bf16[512,1,128]{2,0,1:T(8,128)(2,1)S(1)}, u32[]{:S(2)}, u32[]{:S(2)}) %collective-permute-start) | collective-permute-done | bytes 131104 | tf_op jit(solution)/shard_map/while/body/eval_jaxpr/ppermute | solution.py:21
  179.9 2.0 collective-permute-done.1
  190.0 11.7 %collective-permute-done = bf16[512,1,128]{2,0,1:T(8,128)(2,1)S(1)} collective-permute-done((bf16[512,1,128]{2,0,1:T(8,128)(2,1)}, bf16[512,1,128]{2,0,1:T(8,128)(2,1)S(1)}, u32[]{:S(2)}, u32[]{:S(2)}) %collective-permute-start) | collective-permute-done | bytes 131104 | tf_op jit(solution)/shard_map/while/body/eval_jaxpr/ppermute | solution.py:21
  201.6 2.0 collective-permute-done.1
  211.8 11.7 %collective-permute-done = bf16[512,1,128]{2,0,1:T(8,128)(2,1)S(1)} collective-permute-done((bf16[512,1,128]{2,0,1:T(8,128)(2,1)}, bf16[512,1,128]{2,0,1:T(8,128)(2,1)S(1)}, u32[]{:S(2)}, u32[]{:S(2)}) %collective-permute-start) | collective-permute-done | bytes 131104 | tf_op jit(solution)/shard_map/while/body/eval_jaxpr/ppermute | solution.py:21
  223.4 2.0 collective-permute-done.1
  233.6 11.7 %collective-permute-done = bf16[512,1,128]{2,0,1:T(8,128)(2,1)S(1)} collective-permute-done((bf16[512,1,128]{2,0,1:T(8,128)(2,1)}, bf16[512,1,128]{2,0,1:T(8,128)(2,1)S(1)}, u32[]{:S(2)}, u32[]{:S(2)}) %collective-permute-start) | collective-permute-done | bytes 131104 | tf_op jit(solution)/shard_map/while/body/eval_jaxpr/ppermute | solution.py:21
  255.3 11.7 %collective-permute-done = bf16[512,1,128]{2,0,1:T(8,128)(2,1)S(1)} collective-permute-done((bf16[512,1,128]{2,0,1:T(8,128)(2,1)}, bf16[512,1,128]{2,0,1:T(8,128)(2,1)S(1)}, u32[]{:S(2)}, u32[]{:S(2)}) %collective-permute-start) | collective-permute-done | bytes 131104 | tf_op jit(solution)/shard_map/while/body/eval_jaxpr/ppermute | solution.py:21
  267.0 2.0 collective-permute-done.1
  277.1 11.7 %collective-permute-done = bf16[512,1,128]{2,0,1:T(8,128)(2,1)S(1)} collective-permute-done((bf16[512,1,128]{2,0,1:T(8,128)(2,1)}, bf16[512,1,128]{2,0,1:T(8,128)(2,1)S(1)}, u32[]{:S(2)}, u32[]{:S(2)}) %collective-permute-start) | collective-permute-done | bytes 131104 | tf_op jit(solution)/shard_map/while/body/eval_jaxpr/ppermute | solution.py:21
  288.8 2.0 collective-permute-done.1
  298.9 11.7 %collective-permute-done = bf16[512,1,128]{2,0,1:T(8,128)(2,1)S(1)} collective-permute-done((bf16[512,1,128]{2,0,1:T(8,128)(2,1)}, bf16[512,1,128]{2,0,1:T(8,128)(2,1)S(1)}, u32[]{:S(2)}, u32[]{:S(2)}) %collective-permute-start) | collective-permute-done | bytes 131104 | tf_op jit(solution)/shard_map/while/body/eval_jaxpr/ppermute | solution.py:21
  310.6 2.0 collective-permute-done.1
  320.7 11.7 %collective-permute-done = bf16[512,1,128]{2,0,1:T(8,128)(2,1)S(1)} collective-permute-done((bf16[512,1,128]{2,0,1:T(8,128)(2,1)}, bf16[512,1,128]{2,0,1:T(8,128)(2,1)S(1)}, u32[]{:S(2)}, u32[]{:S(2)}) %collective-permute-start) | collective-permute-done | bytes 131104 | tf_op jit(solution)/shard_map/while/body/eval_jaxpr/ppermute | solution.py:21
  332.4 2.0 collective-permute-done.1
  347.0 12.1 %collective-permute-done.3 = bf16[3,2,1,128]{3,1,2,0:T(2,128)(2,1)S(1)} collective-permute-done((bf16[3,2,1,128]{3,1,2,0:T(2,128)(2,1)S(1)}, bf16[3,2,1,128]{3,1,2,0:T(2,128)(2,1)S(1)}, u32[]{:S(2)}, u32[]{:S(2)}) %collective-permute-start.3) | collective-permute-done | bytes 1568 | tf_op jit(solution)/shard_map/ppermute | solution.py:21
  359.3 3.3 divide_multiply_fusion.1
  363.0 4.9 divide_multiply_fusion
  367.9 2.9 reshape.295
  372.9 3.4 fusion.55
  376.2 4.1 while.55
  382.3 2.3 copy.85
  387.6 130.9 %all-reduce = f32[512]{0:T(512)S(1)} all-reduce(f32[512]{0:T(512)S(1)} %dynamic-update-slice), channel_id=2, replica_groups=mesh['ctx'=32,'tp'=8] {'ctx'}, use_global_device_ids=true, to_apply=%add | all-reduce | flops 512 | bytes 4096
  518.6 72.4 %all-gather.4.cloned.1.call-done = f32[512,64,128]{2,1,0:T(8,128)} async-done(((f32[16,64,128]{2,1,0:T(8,128)}), f32[512,64,128]{2,1,0:T(8,128)}) %all-gather.4.cloned.1.call-update) | async-done | bytes 16777232 | tf_op jit(solution)/shard_map/all_gather | solution.py:26
  591.1 38.6 %while.53 = (s32[]{:T(128)}, f32[16,64,128]{2,1,0:T(8,128)S(1)}, s32[]{:T(128)}, f32[32,16]{1,0:T(8,128)S(1)}, f32[32,16,64,128]{3,2,1,0:T(8,128)}, /*index=5*/s32[]{:T(128)}, s32[]{:T(128)}, s32[]{:T(128)}) while((s32[]{:T(128)}, f32[16,64,128]{2,1,0:T(8,128)S(1)}, s32[]{:T(128)}, f32[32,16]{1,0:T(8,128)S(1)}, ...), condition=%wide.region_21.22_spmd, body=%wide.region_20.21_spmd.sunk | while | flops 262149 | bytes 1573183 | solution.py:34
  629.7 9.7 %fusion.57 = f32[4,16,64,128]{3,2,1,0:T(8,128)S(1)} fusion(f32[4,128,128]{2,1,0:T(8,128)S(1)} %bitcast.191, f32[4,16,64,128]{3,2,1,0:T(8,128)} %get-tuple-element.404, f32[16,64,128]{2,1,0:T(8,128)S(1)} %get-tuple-element.408, f32[4,16]{1,0:T(4,128)S(1)} %get-tuple-element.405), kind=kOutput, calls=%fused_computation.79 | convolution fusion | flops 806354944 | bytes 4980992 | tf_op jit(solution)/shard_map/cihn,chpn->cihp/dot_general | solution.py:232
  639.5 8.6 %fusion.54 = f32[4,128,16,64]{1,3,2,0:T(8,128)S(1)} fusion(f32[4,16,64,128]{3,2,1,0:T(8,128)S(1)} %fusion.57, f32[4,128,16,64]{1,0,3,2:T(4,128)S(1)} %copy-done.2, f32[4,128,16]{1,2,0:T(8,128)S(1)} %copy.77, f32[4,128,16]{1,2,0:T(8,128)S(1)} %copy.74, f32[4,128,128]{2,1,0:T(8,128)S(1)} %copy.72, pred[128,128]{1,0:T(8,128)(4,1)S(1)} %iota_compare_fusion, ...), kind=kOutput, calls=%fused_computation.74 | convolution fusion | flops 812646400 | bytes 6668352 | tf_op jit(solution)/shard_map/cijh,cjhp->cihp/dot_general | solution.py:199
  650.1 14.2 %psum.7 = f32[512]{0:T(512)S(1)} all-reduce(f32[512]{0:T(512)S(1)} %multiply_reduce_fusion), channel_id=1, replica_groups=mesh['ctx'=32,'tp'=8] {'tp'}, use_global_device_ids=true, to_apply=%region_23.24 | all-reduce | flops 512 | bytes 4096 | tf_op jit(solution)/shard_map/psum | solution.py:238
  666.1 2.3 copy.86
  (393 shorter events, 222.8 us)
Async XLA Ops:
  7.2 583.9 %all-gather.4.cloned.1.call-start = ((), (), s32[]{:S(2)}) async-start(), calls=%async_computation | async-start | bytes 17301504 | tf_op jit(solution)/shard_map/all_gather | solution.py:26
  23.1 8.2 %collective-permute-start = (bf16[512,1,128]{2,0,1:T(8,128)(2,1)}, bf16[512,1,128]{2,0,1:T(8,128)(2,1)S(1)}, u32[]{:S(2)}, u32[]{:S(2)}) collective-permute-start(bf16[512,1,128]{2,0,1:T(8,128)(2,1)} %get-tuple-element.738), channel_id=1, source_target_pairs={{0,8},{8,16},{16,24},{24,32},{32,40},{40,48},{48,56},{56,64},{64,7... | collective-permute-start | bytes 393224 | tf_op jit(solution)/shard_map/while/body/eval_jaxpr/ppermute | solution.py:21
  24.4 9.0 %collective-permute-start.1 = (bf16[512,1,128]{2,0,1:T(8,128)(2,1)}, bf16[512,1,128]{2,0,1:T(8,128)(2,1)}, u32[]{:S(2)}, u32[]{:S(2)}) collective-permute-start(bf16[512,1,128]{2,0,1:T(8,128)(2,1)} %get-tuple-element.739), channel_id=1, source_target_pairs={{0,8},{8,16},{16,24},{24,32},{32,40},{40,48},{48,56},{56,64},{64,7... | collective-permute-start | bytes 393224 | tf_op jit(solution)/shard_map/while/body/eval_jaxpr/ppermute | solution.py:21
  43.9 8.3 %collective-permute-start = (bf16[512,1,128]{2,0,1:T(8,128)(2,1)}, bf16[512,1,128]{2,0,1:T(8,128)(2,1)S(1)}, u32[]{:S(2)}, u32[]{:S(2)}) collective-permute-start(bf16[512,1,128]{2,0,1:T(8,128)(2,1)} %get-tuple-element.738), channel_id=1, source_target_pairs={{0,8},{8,16},{16,24},{24,32},{32,40},{40,48},{48,56},{56,64},{64,7... | collective-permute-start | bytes 393224 | tf_op jit(solution)/shard_map/while/body/eval_jaxpr/ppermute | solution.py:21
  45.2 8.7 %collective-permute-start.1 = (bf16[512,1,128]{2,0,1:T(8,128)(2,1)}, bf16[512,1,128]{2,0,1:T(8,128)(2,1)}, u32[]{:S(2)}, u32[]{:S(2)}) collective-permute-start(bf16[512,1,128]{2,0,1:T(8,128)(2,1)} %get-tuple-element.739), channel_id=1, source_target_pairs={{0,8},{8,16},{16,24},{24,32},{32,40},{40,48},{48,56},{56,64},{64,7... | collective-permute-start | bytes 393224 | tf_op jit(solution)/shard_map/while/body/eval_jaxpr/ppermute | solution.py:21
  56.1 15.3 %collective-permute-start = (bf16[512,1,128]{2,0,1:T(8,128)(2,1)}, bf16[512,1,128]{2,0,1:T(8,128)(2,1)S(1)}, u32[]{:S(2)}, u32[]{:S(2)}) collective-permute-start(bf16[512,1,128]{2,0,1:T(8,128)(2,1)} %get-tuple-element.738), channel_id=1, source_target_pairs={{0,8},{8,16},{16,24},{24,32},{32,40},{40,48},{48,56},{56,64},{64,7... | collective-permute-start | bytes 393224 | tf_op jit(solution)/shard_map/while/body/eval_jaxpr/ppermute | solution.py:21
  57.4 15.5 %collective-permute-start.1 = (bf16[512,1,128]{2,0,1:T(8,128)(2,1)}, bf16[512,1,128]{2,0,1:T(8,128)(2,1)}, u32[]{:S(2)}, u32[]{:S(2)}) collective-permute-start(bf16[512,1,128]{2,0,1:T(8,128)(2,1)} %get-tuple-element.739), channel_id=1, source_target_pairs={{0,8},{8,16},{16,24},{24,32},{32,40},{40,48},{48,56},{56,64},{64,7... | collective-permute-start | bytes 393224 | tf_op jit(solution)/shard_map/while/body/eval_jaxpr/ppermute | solution.py:21
  75.2 7.5 %collective-permute-start = (bf16[512,1,128]{2,0,1:T(8,128)(2,1)}, bf16[512,1,128]{2,0,1:T(8,128)(2,1)S(1)}, u32[]{:S(2)}, u32[]{:S(2)}) collective-permute-start(bf16[512,1,128]{2,0,1:T(8,128)(2,1)} %get-tuple-element.738), channel_id=1, source_target_pairs={{0,8},{8,16},{16,24},{24,32},{32,40},{40,48},{48,56},{56,64},{64,7... | collective-permute-start | bytes 393224 | tf_op jit(solution)/shard_map/while/body/eval_jaxpr/ppermute | solution.py:21
  76.5 7.8 %collective-permute-start.1 = (bf16[512,1,128]{2,0,1:T(8,128)(2,1)}, bf16[512,1,128]{2,0,1:T(8,128)(2,1)}, u32[]{:S(2)}, u32[]{:S(2)}) collective-permute-start(bf16[512,1,128]{2,0,1:T(8,128)(2,1)} %get-tuple-element.739), channel_id=1, source_target_pairs={{0,8},{8,16},{16,24},{24,32},{32,40},{40,48},{48,56},{56,64},{64,7... | collective-permute-start | bytes 393224 | tf_op jit(solution)/shard_map/while/body/eval_jaxpr/ppermute | solution.py:21
  86.5 7.1 %collective-permute-start = (bf16[512,1,128]{2,0,1:T(8,128)(2,1)}, bf16[512,1,128]{2,0,1:T(8,128)(2,1)S(1)}, u32[]{:S(2)}, u32[]{:S(2)}) collective-permute-start(bf16[512,1,128]{2,0,1:T(8,128)(2,1)} %get-tuple-element.738), channel_id=1, source_target_pairs={{0,8},{8,16},{16,24},{24,32},{32,40},{40,48},{48,56},{56,64},{64,7... | collective-permute-start | bytes 393224 | tf_op jit(solution)/shard_map/while/body/eval_jaxpr/ppermute | solution.py:21
  87.8 7.8 %collective-permute-start.1 = (bf16[512,1,128]{2,0,1:T(8,128)(2,1)}, bf16[512,1,128]{2,0,1:T(8,128)(2,1)}, u32[]{:S(2)}, u32[]{:S(2)}) collective-permute-start(bf16[512,1,128]{2,0,1:T(8,128)(2,1)} %get-tuple-element.739), channel_id=1, source_target_pairs={{0,8},{8,16},{16,24},{24,32},{32,40},{40,48},{48,56},{56,64},{64,7... | collective-permute-start | bytes 393224 | tf_op jit(solution)/shard_map/while/body/eval_jaxpr/ppermute | solution.py:21
  97.8 7.1 %collective-permute-start = (bf16[512,1,128]{2,0,1:T(8,128)(2,1)}, bf16[512,1,128]{2,0,1:T(8,128)(2,1)S(1)}, u32[]{:S(2)}, u32[]{:S(2)}) collective-permute-start(bf16[512,1,128]{2,0,1:T(8,128)(2,1)} %get-tuple-element.738), channel_id=1, source_target_pairs={{0,8},{8,16},{16,24},{24,32},{32,40},{40,48},{48,56},{56,64},{64,7... | collective-permute-start | bytes 393224 | tf_op jit(solution)/shard_map/while/body/eval_jaxpr/ppermute | solution.py:21
  99.1 7.8 %collective-permute-start.1 = (bf16[512,1,128]{2,0,1:T(8,128)(2,1)}, bf16[512,1,128]{2,0,1:T(8,128)(2,1)}, u32[]{:S(2)}, u32[]{:S(2)}) collective-permute-start(bf16[512,1,128]{2,0,1:T(8,128)(2,1)} %get-tuple-element.739), channel_id=1, source_target_pairs={{0,8},{8,16},{16,24},{24,32},{32,40},{40,48},{48,56},{56,64},{64,7... | collective-permute-start | bytes 393224 | tf_op jit(solution)/shard_map/while/body/eval_jaxpr/ppermute | solution.py:21
  109.1 8.9 %collective-permute-start = (bf16[512,1,128]{2,0,1:T(8,128)(2,1)}, bf16[512,1,128]{2,0,1:T(8,128)(2,1)S(1)}, u32[]{:S(2)}, u32[]{:S(2)}) collective-permute-start(bf16[512,1,128]{2,0,1:T(8,128)(2,1)} %get-tuple-element.738), channel_id=1, source_target_pairs={{0,8},{8,16},{16,24},{24,32},{32,40},{40,48},{48,56},{56,64},{64,7... | collective-permute-start | bytes 393224 | tf_op jit(solution)/shard_map/while/body/eval_jaxpr/ppermute | solution.py:21
  110.4 9.7 %collective-permute-start.1 = (bf16[512,1,128]{2,0,1:T(8,128)(2,1)}, bf16[512,1,128]{2,0,1:T(8,128)(2,1)}, u32[]{:S(2)}, u32[]{:S(2)}) collective-permute-start(bf16[512,1,128]{2,0,1:T(8,128)(2,1)} %get-tuple-element.739), channel_id=1, source_target_pairs={{0,8},{8,16},{16,24},{24,32},{32,40},{40,48},{48,56},{56,64},{64,7... | collective-permute-start | bytes 393224 | tf_op jit(solution)/shard_map/while/body/eval_jaxpr/ppermute | solution.py:21
  122.3 9.2 %collective-permute-start = (bf16[512,1,128]{2,0,1:T(8,128)(2,1)}, bf16[512,1,128]{2,0,1:T(8,128)(2,1)S(1)}, u32[]{:S(2)}, u32[]{:S(2)}) collective-permute-start(bf16[512,1,128]{2,0,1:T(8,128)(2,1)} %get-tuple-element.738), channel_id=1, source_target_pairs={{0,8},{8,16},{16,24},{24,32},{32,40},{40,48},{48,56},{56,64},{64,7... | collective-permute-start | bytes 393224 | tf_op jit(solution)/shard_map/while/body/eval_jaxpr/ppermute | solution.py:21
  123.6 9.9 %collective-permute-start.1 = (bf16[512,1,128]{2,0,1:T(8,128)(2,1)}, bf16[512,1,128]{2,0,1:T(8,128)(2,1)}, u32[]{:S(2)}, u32[]{:S(2)}) collective-permute-start(bf16[512,1,128]{2,0,1:T(8,128)(2,1)} %get-tuple-element.739), channel_id=1, source_target_pairs={{0,8},{8,16},{16,24},{24,32},{32,40},{40,48},{48,56},{56,64},{64,7... | collective-permute-start | bytes 393224 | tf_op jit(solution)/shard_map/while/body/eval_jaxpr/ppermute | solution.py:21
  135.7 9.2 %collective-permute-start = (bf16[512,1,128]{2,0,1:T(8,128)(2,1)}, bf16[512,1,128]{2,0,1:T(8,128)(2,1)S(1)}, u32[]{:S(2)}, u32[]{:S(2)}) collective-permute-start(bf16[512,1,128]{2,0,1:T(8,128)(2,1)} %get-tuple-element.738), channel_id=1, source_target_pairs={{0,8},{8,16},{16,24},{24,32},{32,40},{40,48},{48,56},{56,64},{64,7... | collective-permute-start | bytes 393224 | tf_op jit(solution)/shard_map/while/body/eval_jaxpr/ppermute | solution.py:21
  137.0 9.9 %collective-permute-start.1 = (bf16[512,1,128]{2,0,1:T(8,128)(2,1)}, bf16[512,1,128]{2,0,1:T(8,128)(2,1)}, u32[]{:S(2)}, u32[]{:S(2)}) collective-permute-start(bf16[512,1,128]{2,0,1:T(8,128)(2,1)} %get-tuple-element.739), channel_id=1, source_target_pairs={{0,8},{8,16},{16,24},{24,32},{32,40},{40,48},{48,56},{56,64},{64,7... | collective-permute-start | bytes 393224 | tf_op jit(solution)/shard_map/while/body/eval_jaxpr/ppermute | solution.py:21
  149.2 9.2 %collective-permute-start = (bf16[512,1,128]{2,0,1:T(8,128)(2,1)}, bf16[512,1,128]{2,0,1:T(8,128)(2,1)S(1)}, u32[]{:S(2)}, u32[]{:S(2)}) collective-permute-start(bf16[512,1,128]{2,0,1:T(8,128)(2,1)} %get-tuple-element.738), channel_id=1, source_target_pairs={{0,8},{8,16},{16,24},{24,32},{32,40},{40,48},{48,56},{56,64},{64,7... | collective-permute-start | bytes 393224 | tf_op jit(solution)/shard_map/while/body/eval_jaxpr/ppermute | solution.py:21
  150.5 9.9 %collective-permute-start.1 = (bf16[512,1,128]{2,0,1:T(8,128)(2,1)}, bf16[512,1,128]{2,0,1:T(8,128)(2,1)}, u32[]{:S(2)}, u32[]{:S(2)}) collective-permute-start(bf16[512,1,128]{2,0,1:T(8,128)(2,1)} %get-tuple-element.739), channel_id=1, source_target_pairs={{0,8},{8,16},{16,24},{24,32},{32,40},{40,48},{48,56},{56,64},{64,7... | collective-permute-start | bytes 393224 | tf_op jit(solution)/shard_map/while/body/eval_jaxpr/ppermute | solution.py:21
  162.6 17.3 %collective-permute-start = (bf16[512,1,128]{2,0,1:T(8,128)(2,1)}, bf16[512,1,128]{2,0,1:T(8,128)(2,1)S(1)}, u32[]{:S(2)}, u32[]{:S(2)}) collective-permute-start(bf16[512,1,128]{2,0,1:T(8,128)(2,1)} %get-tuple-element.738), channel_id=1, source_target_pairs={{0,8},{8,16},{16,24},{24,32},{32,40},{40,48},{48,56},{56,64},{64,7... | collective-permute-start | bytes 393224 | tf_op jit(solution)/shard_map/while/body/eval_jaxpr/ppermute | solution.py:21
  163.9 18.0 %collective-permute-start.1 = (bf16[512,1,128]{2,0,1:T(8,128)(2,1)}, bf16[512,1,128]{2,0,1:T(8,128)(2,1)}, u32[]{:S(2)}, u32[]{:S(2)}) collective-permute-start(bf16[512,1,128]{2,0,1:T(8,128)(2,1)} %get-tuple-element.739), channel_id=1, source_target_pairs={{0,8},{8,16},{16,24},{24,32},{32,40},{40,48},{48,56},{56,64},{64,7... | collective-permute-start | bytes 393224 | tf_op jit(solution)/shard_map/while/body/eval_jaxpr/ppermute | solution.py:21
  184.1 17.5 %collective-permute-start = (bf16[512,1,128]{2,0,1:T(8,128)(2,1)}, bf16[512,1,128]{2,0,1:T(8,128)(2,1)S(1)}, u32[]{:S(2)}, u32[]{:S(2)}) collective-permute-start(bf16[512,1,128]{2,0,1:T(8,128)(2,1)} %get-tuple-element.738), channel_id=1, source_target_pairs={{0,8},{8,16},{16,24},{24,32},{32,40},{40,48},{48,56},{56,64},{64,7... | collective-permute-start | bytes 393224 | tf_op jit(solution)/shard_map/while/body/eval_jaxpr/ppermute | solution.py:21
  185.4 18.3 %collective-permute-start.1 = (bf16[512,1,128]{2,0,1:T(8,128)(2,1)}, bf16[512,1,128]{2,0,1:T(8,128)(2,1)}, u32[]{:S(2)}, u32[]{:S(2)}) collective-permute-start(bf16[512,1,128]{2,0,1:T(8,128)(2,1)} %get-tuple-element.739), channel_id=1, source_target_pairs={{0,8},{8,16},{16,24},{24,32},{32,40},{40,48},{48,56},{56,64},{64,7... | collective-permute-start | bytes 393224 | tf_op jit(solution)/shard_map/while/body/eval_jaxpr/ppermute | solution.py:21
  205.9 17.5 %collective-permute-start = (bf16[512,1,128]{2,0,1:T(8,128)(2,1)}, bf16[512,1,128]{2,0,1:T(8,128)(2,1)S(1)}, u32[]{:S(2)}, u32[]{:S(2)}) collective-permute-start(bf16[512,1,128]{2,0,1:T(8,128)(2,1)} %get-tuple-element.738), channel_id=1, source_target_pairs={{0,8},{8,16},{16,24},{24,32},{32,40},{40,48},{48,56},{56,64},{64,7... | collective-permute-start | bytes 393224 | tf_op jit(solution)/shard_map/while/body/eval_jaxpr/ppermute | solution.py:21
  207.2 18.3 %collective-permute-start.1 = (bf16[512,1,128]{2,0,1:T(8,128)(2,1)}, bf16[512,1,128]{2,0,1:T(8,128)(2,1)}, u32[]{:S(2)}, u32[]{:S(2)}) collective-permute-start(bf16[512,1,128]{2,0,1:T(8,128)(2,1)} %get-tuple-element.739), channel_id=1, source_target_pairs={{0,8},{8,16},{16,24},{24,32},{32,40},{40,48},{48,56},{56,64},{64,7... | collective-permute-start | bytes 393224 | tf_op jit(solution)/shard_map/while/body/eval_jaxpr/ppermute | solution.py:21
  227.7 17.5 %collective-permute-start = (bf16[512,1,128]{2,0,1:T(8,128)(2,1)}, bf16[512,1,128]{2,0,1:T(8,128)(2,1)S(1)}, u32[]{:S(2)}, u32[]{:S(2)}) collective-permute-start(bf16[512,1,128]{2,0,1:T(8,128)(2,1)} %get-tuple-element.738), channel_id=1, source_target_pairs={{0,8},{8,16},{16,24},{24,32},{32,40},{40,48},{48,56},{56,64},{64,7... | collective-permute-start | bytes 393224 | tf_op jit(solution)/shard_map/while/body/eval_jaxpr/ppermute | solution.py:21
  229.0 18.3 %collective-permute-start.1 = (bf16[512,1,128]{2,0,1:T(8,128)(2,1)}, bf16[512,1,128]{2,0,1:T(8,128)(2,1)}, u32[]{:S(2)}, u32[]{:S(2)}) collective-permute-start(bf16[512,1,128]{2,0,1:T(8,128)(2,1)} %get-tuple-element.739), channel_id=1, source_target_pairs={{0,8},{8,16},{16,24},{24,32},{32,40},{40,48},{48,56},{56,64},{64,7... | collective-permute-start | bytes 393224 | tf_op jit(solution)/shard_map/while/body/eval_jaxpr/ppermute | solution.py:21
  249.5 17.5 %collective-permute-start = (bf16[512,1,128]{2,0,1:T(8,128)(2,1)}, bf16[512,1,128]{2,0,1:T(8,128)(2,1)S(1)}, u32[]{:S(2)}, u32[]{:S(2)}) collective-permute-start(bf16[512,1,128]{2,0,1:T(8,128)(2,1)} %get-tuple-element.738), channel_id=1, source_target_pairs={{0,8},{8,16},{16,24},{24,32},{32,40},{40,48},{48,56},{56,64},{64,7... | collective-permute-start | bytes 393224 | tf_op jit(solution)/shard_map/while/body/eval_jaxpr/ppermute | solution.py:21
  250.8 18.3 %collective-permute-start.1 = (bf16[512,1,128]{2,0,1:T(8,128)(2,1)}, bf16[512,1,128]{2,0,1:T(8,128)(2,1)}, u32[]{:S(2)}, u32[]{:S(2)}) collective-permute-start(bf16[512,1,128]{2,0,1:T(8,128)(2,1)} %get-tuple-element.739), channel_id=1, source_target_pairs={{0,8},{8,16},{16,24},{24,32},{32,40},{40,48},{48,56},{56,64},{64,7... | collective-permute-start | bytes 393224 | tf_op jit(solution)/shard_map/while/body/eval_jaxpr/ppermute | solution.py:21
  271.3 17.5 %collective-permute-start = (bf16[512,1,128]{2,0,1:T(8,128)(2,1)}, bf16[512,1,128]{2,0,1:T(8,128)(2,1)S(1)}, u32[]{:S(2)}, u32[]{:S(2)}) collective-permute-start(bf16[512,1,128]{2,0,1:T(8,128)(2,1)} %get-tuple-element.738), channel_id=1, source_target_pairs={{0,8},{8,16},{16,24},{24,32},{32,40},{40,48},{48,56},{56,64},{64,7... | collective-permute-start | bytes 393224 | tf_op jit(solution)/shard_map/while/body/eval_jaxpr/ppermute | solution.py:21
  272.5 18.3 %collective-permute-start.1 = (bf16[512,1,128]{2,0,1:T(8,128)(2,1)}, bf16[512,1,128]{2,0,1:T(8,128)(2,1)}, u32[]{:S(2)}, u32[]{:S(2)}) collective-permute-start(bf16[512,1,128]{2,0,1:T(8,128)(2,1)} %get-tuple-element.739), channel_id=1, source_target_pairs={{0,8},{8,16},{16,24},{24,32},{32,40},{40,48},{48,56},{56,64},{64,7... | collective-permute-start | bytes 393224 | tf_op jit(solution)/shard_map/while/body/eval_jaxpr/ppermute | solution.py:21
  293.0 17.5 %collective-permute-start = (bf16[512,1,128]{2,0,1:T(8,128)(2,1)}, bf16[512,1,128]{2,0,1:T(8,128)(2,1)S(1)}, u32[]{:S(2)}, u32[]{:S(2)}) collective-permute-start(bf16[512,1,128]{2,0,1:T(8,128)(2,1)} %get-tuple-element.738), channel_id=1, source_target_pairs={{0,8},{8,16},{16,24},{24,32},{32,40},{40,48},{48,56},{56,64},{64,7... | collective-permute-start | bytes 393224 | tf_op jit(solution)/shard_map/while/body/eval_jaxpr/ppermute | solution.py:21
  294.3 18.3 %collective-permute-start.1 = (bf16[512,1,128]{2,0,1:T(8,128)(2,1)}, bf16[512,1,128]{2,0,1:T(8,128)(2,1)}, u32[]{:S(2)}, u32[]{:S(2)}) collective-permute-start(bf16[512,1,128]{2,0,1:T(8,128)(2,1)} %get-tuple-element.739), channel_id=1, source_target_pairs={{0,8},{8,16},{16,24},{24,32},{32,40},{40,48},{48,56},{56,64},{64,7... | collective-permute-start | bytes 393224 | tf_op jit(solution)/shard_map/while/body/eval_jaxpr/ppermute | solution.py:21
  314.8 17.5 %collective-permute-start = (bf16[512,1,128]{2,0,1:T(8,128)(2,1)}, bf16[512,1,128]{2,0,1:T(8,128)(2,1)S(1)}, u32[]{:S(2)}, u32[]{:S(2)}) collective-permute-start(bf16[512,1,128]{2,0,1:T(8,128)(2,1)} %get-tuple-element.738), channel_id=1, source_target_pairs={{0,8},{8,16},{16,24},{24,32},{32,40},{40,48},{48,56},{56,64},{64,7... | collective-permute-start | bytes 393224 | tf_op jit(solution)/shard_map/while/body/eval_jaxpr/ppermute | solution.py:21
  316.1 18.3 %collective-permute-start.1 = (bf16[512,1,128]{2,0,1:T(8,128)(2,1)}, bf16[512,1,128]{2,0,1:T(8,128)(2,1)}, u32[]{:S(2)}, u32[]{:S(2)}) collective-permute-start(bf16[512,1,128]{2,0,1:T(8,128)(2,1)} %get-tuple-element.739), channel_id=1, source_target_pairs={{0,8},{8,16},{16,24},{24,32},{32,40},{40,48},{48,56},{56,64},{64,7... | collective-permute-start | bytes 393224 | tf_op jit(solution)/shard_map/while/body/eval_jaxpr/ppermute | solution.py:21
  336.6 7.2 %copy-start.12 = (f32[4,1024]{1,0:T(4,128)S(1)}, f32[4,1024]{1,0:T(4,128)}, u32[]{:S(2)}) copy-start(f32[4,1024]{1,0:T(4,128)} %param.33) | copy-start | bytes 49156
  336.6 7.3 %copy-start.11 = (f32[512,16]{0,1:T(8,128)S(1)}, f32[512,16]{0,1:T(8,128)}, u32[]{:S(2)}) copy-start(f32[512,16]{0,1:T(8,128)} %param.29) | copy-start | bytes 98308
  336.6 7.3 %copy-start.18 = (f32[16]{0:T(128)S(1)}, f32[16]{0:T(128)}, u32[]{:S(2)}) copy-start(f32[16]{0:T(128)} %param.31) | copy-start | bytes 196
  336.6 7.3 %copy-start.19 = (f32[16]{0:T(128)S(1)}, f32[16]{0:T(128)}, u32[]{:S(2)}) copy-start(f32[16]{0:T(128)} %param.30) | copy-start | bytes 196
  336.7 7.9 %copy-start.16 = (f32[4,2,1,128]{3,2,1,0:T(1,128)S(1)}, f32[4,2,1,128]{3,2,1,0:T(1,128)}, u32[]{:S(2)}) copy-start(f32[4,2,1,128]{3,2,1,0:T(1,128)} %param.34) | copy-start | bytes 12292
  340.0 23.0 %collective-permute-start.2 = (bf16[3,1024]{0,1:T(8,128)(2,1)}, bf16[3,1024]{0,1:T(8,128)(2,1)}, u32[]{:S(2)}, u32[]{:S(2)}) collective-permute-start(bf16[3,1024]{0,1:T(8,128)(2,1)} %bitcast.38), channel_id=1, source_target_pairs={{0,8},{8,16},{16,24},{24,32},{32,40},{40,48},{48,56},{56,64},{64,7... | collective-permute-start | bytes 18440 | tf_op jit(solution)/shard_map/ppermute | solution.py:21
  341.3 17.7 %collective-permute-start.3 = (bf16[3,2,1,128]{3,1,2,0:T(2,128)(2,1)S(1)}, bf16[3,2,1,128]{3,1,2,0:T(2,128)(2,1)S(1)}, u32[]{:S(2)}, u32[]{:S(2)}) collective-permute-start(bf16[3,2,1,128]{3,1,2,0:T(2,128)(2,1)S(1)} %slice.120), channel_id=1, source_target_pairs={{0,8},{8,16},{16,24},{24,32},{32,40},{40,48},{48,56},{56,64},{64,7... | collective-permute-start | bytes 4616 | tf_op jit(solution)/shard_map/ppermute | solution.py:21
  346.8 21.1 %copy-start.1 = (bf16[512,1,8,128]{0,3,2,1:T(8,128)(2,1)}, bf16[512,1,8,128]{0,3,2,1:T(8,128)(2,1)S(1)}, u32[]{:S(2)}) copy-start(bf16[512,1,8,128]{0,3,2,1:T(8,128)(2,1)S(1)} %copy.70) | copy-start | bytes 3145732
  629.7 9.7 %copy-start.2 = (f32[4,128,16,64]{1,0,3,2:T(4,128)S(1)}, f32[4,128,16,64]{1,0,3,2:T(4,128)}, u32[]{:S(2)}) copy-start(f32[4,128,16,64]{1,0,3,2:T(4,128)} %reshape.295) | copy-start | bytes 6291460
  629.7 9.7 %copy-start.20 = (f32[16]{0:T(128)S(1)}, f32[16]{0:T(128)}, u32[]{:S(2)}) copy-start(f32[16]{0:T(128)} %param.32) | copy-start | bytes 196
  649.4 14.9 %copy-start.15 = (f32[1024]{0:T(1024)S(1)}, f32[1024]{0:T(1024)}, u32[]{:S(2)}) copy-start(f32[1024]{0:T(1024)} %param.35) | copy-start | bytes 12292
  (13 other events, 43.0 us)
Sparse Core Ops, SparseCore 0:
  381.3 209.6 all-gather.3
where the time goes:
time: 680 us; the launch traced here: 675 us
  waiting for transfers between devices  244 us (36%)
  blocking collectives  145 us (21%)
  other arithmetic  113 us (17%)
  local copies, waits for them, and re-layouts  61.5 us (9%)
  starting transfers between devices  49.1 us (7%)
  matrix products  32.8 us (5%)
  between operations  15.8 us (2%)
  loops' own time  14 us (2%)
    ppermute x38, waiting for transfers between devices, from_behind(): lax.ppermute(value, axis, [(source, source + steps) for source in range(l...  172 us
    unnamed x1, blocking collectives  131 us
    all_gather x1, waiting for transfers between devices, prefix_2(): gathered = jax.tree.map(lambda a: lax.all_gather(a, axis), part)  72.4 us
    ppermute x38, starting transfers between devices, from_behind(): lax.ppermute(value, axis, [(source, source + steps) for source in range(l...  49.1 us
    while x36, local copies, waits for them, and re-layouts  40 us
    add x31, other arithmetic, chain_states(): later[0][:, None, None] * earlier[1] + later[1]  36.8 us
    reduce_or x18, other arithmetic, attend_block(): return lax.cond(jnp.any(allowed), update, lambda running: running, carried)  31.6 us
    reduce_sum x21, other arithmetic, token_segments(): return jnp.sum(reached * increments[None, :], axis=1)  17.7 us
  transfers between devices with their start and end apart: 39, of which 38 were waited for; matrix products, arithmetic and copies ran while one was open for 9% of the time, Pallas kernels for 0%

commit v1 on v0

v1 whole, which is shorter than its diff:
```python
import functools
import math

import jax
import jax.numpy as jnp
from jax import lax
from jax.experimental import pallas as pl
from jax.experimental.pallas import tpu as pltpu
from jax.sharding import PartitionSpec as P

BLOCK = 128
NCTX = 32
NX = 4
NZ = 8
NTP = 8
ROWS = 512
HEADS = 8
HEAD_DIM = 128
SSM_HEADS = 16
SSM_DIM = 64
CHANNELS = 1024
STATE = 128
CHUNKS = ROWS // BLOCK
ALL_CHANNELS = 8192
NORM_EPS = 1e-05
EXP_SCALE = math.log2(math.e) / math.sqrt(HEAD_DIM)
HOPS = 6
FOLD_ORDER = (
    (1, 0), (0, 1), (2, 0), (0, 3), (0, 2),
    (1, 1), (3, 0), (1, 3), (1, 2),
    (2, 1), (4, 0), (2, 3), (2, 2),
    (3, 1), (3, 3), (3, 2),
    (4, 1), (4, 2),
)
Z_STEP = {1: 0, 2: 2, 3: 4, 4: 7, 5: 11}
X_STEP = {0: 0, 1: 1, 2: 5, 3: 9, 4: 13, 5: 16}
H_STEP = {0: 4, 1: 4, 2: 8, 3: 12, 4: 15, 5: 17}

f32 = jnp.float32
bf16 = jnp.bfloat16
HIGHEST = lax.Precision.HIGHEST


def dot(a, b, ca=1, cb=0, precision=None):
    return lax.dot_general(
        a, b, (((ca,), (cb,)), ((), ())), precision=precision, preferred_element_type=f32
    )


def remote(src, dst, send_sem, recv_sem, device):
    return pltpu.make_async_remote_copy(
        src_ref=src,
        dst_ref=dst,
        send_sem=send_sem,
        recv_sem=recv_sem,
        device_id=device,
        device_id_type=pl.DeviceIdType.MESH,
    )


def pick(table, n):
    value = jnp.int32(table[0])
    for i in range(1, len(table)):
        value = jnp.where(n >= i, jnp.int32(table[i]), value)
    return value


def attention_kernel(
    seg_ref, qt_ref, kv_ref, out_ref,
    slots, m_s, l_s, acc_s,
    send_z, send_p, send_m, send_a, send_b,
    recv_z, recv_p, recv_m, recv_a, recv_b,
):
    me = lax.axis_index("ctx")
    z, x = me // NX, me % NX
    up = {"ctx": lax.rem(z + 1, NZ) * NX + x}
    down = {"ctx": lax.rem(z + NZ - 1, NZ) * NX + x}
    right = {"ctx": z * NX + lax.rem(x + 1, NX)}
    left = {"ctx": z * NX + lax.rem(x + NX - 1, NX)}

    barrier = pltpu.get_barrier_semaphore()
    for peer in (up, down, right, left):
        pl.semaphore_signal(barrier, inc=1, device_id=peer, device_id_type=pl.DeviceIdType.MESH)
    pl.semaphore_wait(barrier, 4)

    half = kv_ref.shape[0] // 2

    def column(k):
        return kv_ref if k == 0 else slots.at[k, 0]

    def copy_z(k):
        return remote(column(k), slots.at[k + 1, 0], send_z.at[k], recv_z.at[k + 1], up)

    def copy_p(k):
        return remote(column(k), slots.at[k, 1], send_p.at[k], recv_p.at[k], right)

    def copy_m(k):
        return remote(column(k), slots.at[k, 3], send_m.at[k], recv_m.at[k], left)

    def copy_a(k):
        return remote(
            slots.at[k, 1, pl.ds(0, half)], slots.at[k, 2, pl.ds(0, half)],
            send_a.at[k], recv_a.at[k], right,
        )

    def copy_b(k):
        return remote(
            slots.at[k, 3, pl.ds(half, half)], slots.at[k, 2, pl.ds(half, half)],
            send_b.at[k], recv_b.at[k], left,
        )

    def z_step(k):
        if k > 0:
            copy_z(k - 1).wait_recv()
        if k < HOPS - 1:
            copy_z(k).start()
        copy_p(k).start()
        copy_m(k).start()

    def x_step(k):
        copy_p(k).wait_recv()
        copy_a(k).start()
        copy_m(k).wait_recv()
        copy_b(k).start()

    def h_step(k):
        copy_a(k).wait_recv()
        copy_b(k).wait_recv()

    z_step(0)

    def scores(k, qb, hp):
        return dot(k, qt_ref[qb, :, hp * 256 : (hp + 1) * 256])

    own_seg = [seg_ref[me * CHUNKS + c] for c in range(CHUNKS)]
    key_pos = lax.broadcasted_iota(jnp.int32, (BLOCK, 256), 0)
    query_pos = lax.broadcasted_iota(jnp.int32, (BLOCK, 256), 1) % BLOCK
    causal = key_pos <= query_pos
    tiles = [(qb, hp) for qb in range(CHUNKS) for hp in range(4)]

    def own_soft(qb, s):
        pens = [jnp.where(own_seg[b] == own_seg[qb], 0.0, 1e30).astype(f32) for b in range(qb)]
        last = jnp.where(causal, s[qb * BLOCK :], -1e30)
        m = jnp.max(last, axis=0, keepdims=True) * EXP_SCALE
        for b in range(qb):
            top = jnp.max(s[b * BLOCK : (b + 1) * BLOCK], axis=0, keepdims=True)
            m = jnp.maximum(m, top * EXP_SCALE - pens[b])
        total = jnp.zeros_like(m)
        parts = []
        for b in range(qb + 1):
            if b < qb:
                p = jnp.exp2(s[b * BLOCK : (b + 1) * BLOCK] * EXP_SCALE - (m + pens[b]))
            else:
                p = jnp.where(causal, jnp.exp2(last * EXP_SCALE - m), 0.0)
            total = total + jnp.sum(p, axis=0, keepdims=True)
            parts.append(p.astype(bf16))
        return m, total, jnp.concatenate(parts, axis=0)

    def values(block, count):
        return jnp.concatenate(
            [block[half + b * BLOCK : half + (b + 1) * BLOCK] for b in range(count)], axis=1
        )

    def own_fold(t, m, total, p):
        qb, hp = t
        i = qb * 4 + hp
        m_s[i] = m
        l_s[i] = total
        acc_s[i] = dot(values(kv_ref, qb + 1), p)

    s_now = scores(kv_ref[0:BLOCK], 0, 0)
    waiting = None
    for n, t in enumerate(tiles):
        s_next = None
        if n + 1 < len(tiles):
            qb, hp = tiles[n + 1]
            s_next = scores(kv_ref[0 : (qb + 1) * BLOCK], qb, hp)
        done = own_soft(t[0], s_now)
        if waiting is not None:
            own_fold(waiting[0], *waiting[1])
        waiting = (t, done)
        s_now = s_next
    own_fold(waiting[0], *waiting[1])

    def soft(i, s, pens):
        m = m_s[i]
        new = m
        for b in range(CHUNKS):
            top = jnp.max(s[b * BLOCK : (b + 1) * BLOCK], axis=0, keepdims=True)
            new = jnp.maximum(new, top * EXP_SCALE - pens[b])
        total = jnp.zeros_like(m)
        parts = []
        for b in range(CHUNKS):
            p = jnp.exp2(s[b * BLOCK : (b + 1) * BLOCK] * EXP_SCALE - (new + pens[b]))
            total = total + jnp.sum(p, axis=0, keepdims=True)
            parts.append(p.astype(bf16))
        shrink = jnp.exp2(m - new)
        m_s[i] = new
        l_s[i] = l_s[i] * shrink + total
        return shrink, jnp.concatenate(parts, axis=0)

    def fold_block(n, carry):
        for k in range(HOPS):
            if k in Z_STEP:
                pl.when(n == Z_STEP[k])(functools.partial(z_step, k))
            pl.when(n == X_STEP[k])(functools.partial(x_step, k))
        for k in range(HOPS):
            pl.when(n == H_STEP[k])(functools.partial(h_step, k))
        rank = pick([o[0] for o in FOLD_ORDER], n)
        col = pick([o[1] for o in FOLD_ORDER], n)
        source = me - (NX * rank + col)
        k = jnp.where(x >= col, rank, rank + 1)
        first = jnp.maximum(source, 0) * CHUNKS
        key_seg = [seg_ref[first + b] for b in range(CHUNKS)]
        pens = [
            [
                jnp.where((source >= 0) & (key_seg[b] == own_seg[qb]), 0.0, 1e30).astype(f32)
                for b in range(CHUNKS)
            ]
            for qb in range(CHUNKS)
        ]
        keys = slots[k, col, 0:half]
        vt = jnp.concatenate(
            [slots[k, col, half + b * BLOCK : half + (b + 1) * BLOCK] for b in range(CHUNKS)],
            axis=1,
        )

        def fold(t, shrink, p):
            i = t[0] * 4 + t[1]
            acc_s[i] = acc_s[i] * shrink + dot(vt, p)

        s_now = scores(keys, 0, 0)
        waiting = None
        for n_tile, t in enumerate(tiles):
            s_next = scores(keys, *tiles[n_tile + 1]) if n_tile + 1 < len(tiles) else None
            done = soft(t[0] * 4 + t[1], s_now, pens[t[0]])
            if waiting is not None:
                fold(waiting[0], *waiting[1])
            waiting = (t, done)
            s_now = s_next
        fold(waiting[0], *waiting[1])
        return carry

    lax.fori_loop(0, len(FOLD_ORDER), fold_block, 0)

    for qb, hp in tiles:
        i = qb * 4 + hp
        o = acc_s[i] / l_s[i]
        for j in range(2):
            c = (hp * 2 + j) * HEAD_DIM
            part = o[:, j * BLOCK : (j + 1) * BLOCK].T
            out_ref[qb * BLOCK : (qb + 1) * BLOCK, c : c + HEAD_DIM] = part.astype(bf16)

    for k in range(HOPS):
        if k < HOPS - 1:
            copy_z(k).wait_send()
        copy_p(k).wait_send()
        copy_m(k).wait_send()
        copy_a(k).wait_send()
        copy_b(k).wait_send()


def attention(segments, qt, kv):
    dma = pltpu.SemaphoreType.DMA
    return pl.pallas_call(
        attention_kernel,
        out_shape=jax.ShapeDtypeStruct((ROWS, CHANNELS), bf16),
        in_specs=[
            pl.BlockSpec(memory_space=pltpu.SMEM),
            pl.BlockSpec(memory_space=pltpu.VMEM),
            pl.BlockSpec(memory_space=pltpu.VMEM),
        ],
        out_specs=pl.BlockSpec(memory_space=pltpu.VMEM),
        scratch_shapes=[
            pltpu.VMEM((HOPS, NX, 2 * ROWS, HEAD_DIM), bf16),
            pltpu.VMEM((16, 1, 256), f32),
            pltpu.VMEM((16, 1, 256), f32),
            pltpu.VMEM((16, HEAD_DIM, 256), f32),
        ]
        + [dma((HOPS,))] * 10,
        compiler_params=pltpu.CompilerParams(
            collective_id=0, has_side_effects=True, vmem_limit_bytes=56 << 20
        ),
        cost_estimate=pl.CostEstimate(
            flops=20 * 10**9, bytes_accessed=4 << 20, transcendentals=40 * 10**6
        ),
        name="attention",
    )(segments, qt, kv)


def silu(v):
    return v / (1.0 + jnp.exp(-v))


def softplus(v):
    return jnp.maximum(v, 0.0) + jnp.log1p(jnp.exp(-jnp.abs(v)))


def split(v):
    high = v.astype(bf16)
    return high, (v - high.astype(f32)).astype(bf16)


def spread(v, expand):
    high, low = split(v)
    return dot(high, expand) + dot(low, expand)


def mixer_kernel(
    seg_ref, att_ref, gate_ref, proj_ref, step_ref, step_t_ref, bias_ref, bias_t_ref,
    rate_ref, rate_t_ref, skip_ref, tap_ref, tap_state_ref, gain_ref, out_ref,
    halo_a, halo_s, ext, ext_s, xs, cs, ys, gs, enter,
    t_send, t_all, s_send, s_in, p_send, p_in, q_all,
    halo_sems, t_sems, s_sems, p_sems, q_sems,
    halo_recv, t_recv, s_recv, p_recv, q_recv,
):
    me = lax.axis_index("ctx")
    tp = lax.axis_index("tp")
    mesh_id = pl.DeviceIdType.MESH
    barrier = pltpu.get_barrier_semaphore()

    def greet_ctx(o, c):
        pl.semaphore_signal(
            barrier, inc=1, device_id={"ctx": lax.rem(me + o, NCTX)}, device_id_type=mesh_id
        )
        return c

    def greet_tp(o, c):
        pl.semaphore_signal(
            barrier, inc=1, device_id={"tp": lax.rem(tp + o, NTP)}, device_id_type=mesh_id
        )
        return c

    lax.fori_loop(1, NCTX, greet_ctx, 0)
    lax.fori_loop(1, NTP, greet_tp, 0)

    iota_r = lax.broadcasted_iota(jnp.int32, (BLOCK, BLOCK), 0)
    iota_c = lax.broadcasted_iota(jnp.int32, (BLOCK, BLOCK), 1)
    lower = iota_r >= iota_c
    tri = jnp.where(lower, 1.0, 0.0).astype(f32)
    expand = jnp.where(
        lax.broadcasted_iota(jnp.int32, (SSM_HEADS, CHANNELS), 1) // SSM_DIM
        == lax.broadcasted_iota(jnp.int32, (SSM_HEADS, CHANNELS), 0),
        1.0,
        0.0,
    ).astype(bf16)
    keep = []
    for c in range(CHUNKS):
        at = me * CHUNKS + c
        same = (at > 0) & (seg_ref[at] == seg_ref[jnp.maximum(at - 1, 0)])
        keep.append(jnp.where(same, 1.0, 0.0).astype(f32))
    dt, dt_t, cum, cum_t = [], [], [], []
    for c in range(CHUNKS):
        rows = slice(c * BLOCK, (c + 1) * BLOCK)
        d = softplus(step_ref[rows, :] + bias_ref[...])
        d_t = softplus(step_t_ref[:, rows] + bias_t_ref[...])
        dt.append(d)
        dt_t.append(d_t)
        cum.append(dot(tri, -d * rate_ref[...], precision=HIGHEST))
        cum_t.append(dot(-d_t * rate_t_ref[...], tri, 1, 1, precision=HIGHEST))
    last = [v[BLOCK - 1 : BLOCK, :] for v in cum]
    factor = [keep[c] * jnp.exp(last[c]) for c in range(CHUNKS)]
    prefix = [jnp.ones_like(last[0])]
    for c in range(CHUNKS):
        prefix.append(prefix[-1] * factor[c])
    t_send[...] = jnp.zeros_like(t_send)
    t_send[0:1, 0:SSM_HEADS] = prefix[CHUNKS]

    pl.semaphore_wait(barrier, NCTX - 1 + NTP - 1)

    tail = ROWS - 16
    following = {"ctx": lax.rem(me + 1, NCTX)}
    send_att = remote(
        att_ref.at[pl.ds(tail, 16)], halo_a, halo_sems.at[0], halo_recv.at[0], following
    )
    send_proj = remote(
        proj_ref.at[pl.ds(tail, 16)], halo_s, halo_sems.at[1], halo_recv.at[1], following
    )
    send_att.start()
    send_proj.start()

    def t_copy(o, slot):
        return remote(
            t_send, t_all.at[slot], t_sems.at[o], t_recv.at[slot], {"ctx": lax.rem(me + o, NCTX)}
        )

    def s_copy(o, slot):
        to = lax.rem(me + o, NCTX)
        return remote(s_send.at[to], s_in.at[slot], s_sems.at[o], s_recv.at[slot], {"ctx": to})

    def p_copy(o, slot):
        to = lax.rem(me + o, NCTX)
        return remote(p_send.at[to], p_in.at[slot], p_sems.at[o], p_recv.at[slot], {"ctx": to})

    def q_copy(o, slot):
        return remote(
            q_all.at[tp], q_all.at[slot], q_sems.at[o], q_recv.at[slot],
            {"tp": lax.rem(tp + o, NTP)},
        )

    def start_all(copy, count, place):
        def one(o, c):
            copy(o, place).start()
            return c

        lax.fori_loop(1, count, one, 0)

    def recv_all(copy, count, place):
        def one(o, c):
            copy(o, lax.rem(place + o, count)).wait_recv()
            return c

        lax.fori_loop(1, count, one, 0)

    def sent_all(copy, count, place):
        def one(o, c):
            copy(o, place).wait_send()
            return c

        lax.fori_loop(1, count, one, 0)

    start_all(t_copy, NCTX, me)
    t_all[me] = t_send[...]

    send_att.wait_recv()
    send_proj.wait_recv()

    state = jnp.zeros((STATE, CHANNELS), f32)
    for c in range(CHUNKS):
        rows = slice(c * BLOCK, (c + 1) * BLOCK)
        if c == 0:
            ext[0:8] = halo_a[...].astype(f32)[8:16] * keep[c]
            ext_s[0:8] = halo_s[...].astype(f32)[8:16] * keep[c]
        else:
            before = slice(c * BLOCK - 16, c * BLOCK)
            ext[0:8] = att_ref[before, :].astype(f32)[8:16] * keep[c]
            ext_s[0:8] = proj_ref[before, :].astype(f32)[8:16] * keep[c]
        ext[8:] = att_ref[rows, :].astype(f32)
        ext_s[8:] = proj_ref[rows, :].astype(f32)
        conv = tap_ref[0:1, :] * ext[8 : 8 + BLOCK]
        conv_s = tap_state_ref[0:1, :] * ext_s[8 : 8 + BLOCK]
        for k in range(1, 4):
            conv = conv + tap_ref[k : k + 1, :] * ext[8 - k : 8 - k + BLOCK]
            conv_s = conv_s + tap_state_ref[k : k + 1, :] * ext_s[8 - k : 8 - k + BLOCK]
        conv = silu(conv)
        conv_s = silu(conv_s)
        xs[rows, :] = conv
        cs[rows, :] = conv_s
        enter[c] = state.astype(bf16)
        to_end = jnp.exp(last[c] - cum[c]) * dt[c]
        scaled = (conv * spread(to_end, expand)).astype(bf16)
        write_t = conv_s[:, 0:STATE].T.astype(bf16)
        pair = jnp.concatenate([factor[c], jnp.zeros((7, SSM_HEADS), f32)], axis=0)
        state = state * spread(pair, expand)[0:1] + dot(write_t, scaled)

    for ng in range(8):
        for cg in range(4):
            s_send[ng * 4 + cg] = state[
                ng * 16 : (ng + 1) * 16, cg * 256 : (cg + 1) * 256
            ].astype(bf16)
    start_all(s_copy, NCTX, me)
    s_in[me] = s_send[me]

    low_half = lax.broadcasted_iota(jnp.int32, (BLOCK, BLOCK), 1) < SSM_DIM
    for c in range(CHUNKS):
        rows = slice(c * BLOCK, (c + 1) * BLOCK)
        write = cs[rows, 0:STATE]
        read = cs[rows, STATE:]
        meet = dot(read, write, 1, 1, precision=HIGHEST)
        conv = xs[rows, :]
        begin = spread(jnp.exp(cum[c]) * keep[c], expand)
        out = dot(read.astype(bf16), enter[c]) * begin + conv * skip_ref[...]
        parts = []
        for pair in range(SSM_HEADS // 2):
            mixes = []
            for h in (2 * pair, 2 * pair + 1):
                gap = cum[c][:, h : h + 1] - cum_t[c][h : h + 1, :]
                mix = jnp.exp(jnp.where(lower, gap, 0.0)) * meet * dt_t[c][h : h + 1, :]
                mixes.append(jnp.where(lower, mix, 0.0).astype(bf16))
            both = conv[:, pair * BLOCK : (pair + 1) * BLOCK]
            stacked = jnp.concatenate(
                [jnp.where(low_half, both, 0.0), jnp.where(low_half, 0.0, both)], axis=0
            ).astype(bf16)
            parts.append(dot(jnp.concatenate(mixes, axis=1), stacked))
        ys[rows, :] = out + jnp.concatenate(parts, axis=1)

    recv_all(t_copy, NCTX, me)
    share = lax.rem(me, 4)
    expand_share = jnp.where(
        lax.broadcasted_iota(jnp.int32, (BLOCK, 256), 1) // SSM_DIM + share * 4
        == lax.broadcasted_iota(jnp.int32, (BLOCK, 256), 0),
        1.0,
        0.0,
    ).astype(bf16)
    decays = spread(t_all[:, 0, :], expand_share)
    recv_all(s_copy, NCTX, me)
    running = jnp.zeros((16, 256), f32)
    for d in range(NCTX):
        p_send[d] = running.astype(bf16)
        running = running * decays[d : d + 1, :] + s_in[d].astype(f32)
    start_all(p_copy, NCTX, me)
    p_in[me] = p_send[me]

    for c in range(CHUNKS):
        rows = slice(c * BLOCK, (c + 1) * BLOCK)
        gs[rows, :] = silu(gate_ref[rows, :].astype(f32))

    recv_all(p_copy, NCTX, me)
    incoming = jnp.concatenate(
        [
            jnp.concatenate([p_in[ng * 4 + cg] for cg in range(4)], axis=1)
            for ng in range(8)
        ],
        axis=0,
    )
    squares = []
    for c in range(CHUNKS):
        rows = slice(c * BLOCK, (c + 1) * BLOCK)
        begin = spread(jnp.exp(cum[c]) * (prefix[c] * keep[c]), expand)
        out = ys[rows, :] + dot(cs[rows, STATE:].astype(bf16), incoming) * begin
        gated = out * gs[rows, :]
        gs[rows, :] = gated
        sq = gated * gated
        folded = sq[:, 0:BLOCK]
        for i in range(1, CHANNELS // BLOCK):
            folded = folded + sq[:, i * BLOCK : (i + 1) * BLOCK]
        squares.append(jnp.sum(folded.T, axis=0, keepdims=True))
    squares.append(jnp.zeros((8 - CHUNKS, BLOCK), f32))
    q_all[tp] = jnp.concatenate(squares, axis=0)
    start_all(q_copy, NTP, tp)
    recv_all(q_copy, NTP, tp)
    total = q_all[0]
    for i in range(1, NTP):
        total = total + q_all[i]
    scale = lax.rsqrt(total * (1.0 / ALL_CHANNELS) + NORM_EPS)
    for c in range(CHUNKS):
        rows = slice(c * BLOCK, (c + 1) * BLOCK)
        by_row = jnp.broadcast_to(scale[c : c + 1, :], (BLOCK, BLOCK)).T
        for i in range(CHANNELS // BLOCK):
            cols = slice(i * BLOCK, (i + 1) * BLOCK)
            out_ref[rows, cols] = (gs[rows, cols] * gain_ref[:, cols] * by_row).astype(bf16)

    send_att.wait_send()
    send_proj.wait_send()
    sent_all(t_copy, NCTX, me)
    sent_all(s_copy, NCTX, me)
    sent_all(p_copy, NCTX, me)
    sent_all(q_copy, NTP, tp)


def mixer(segments, *arrays):
    dma = pltpu.SemaphoreType.DMA
    vmem = pltpu.VMEM
    return pl.pallas_call(
        mixer_kernel,
        out_shape=jax.ShapeDtypeStruct((ROWS, CHANNELS), bf16),
        in_specs=[pl.BlockSpec(memory_space=pltpu.SMEM)]
        + [pl.BlockSpec(memory_space=pltpu.VMEM)] * len(arrays),
        out_specs=pl.BlockSpec(memory_space=pltpu.VMEM),
        scratch_shapes=[
            vmem((16, CHANNELS), bf16),
            vmem((16, 2 * STATE), bf16),
            vmem((8 + BLOCK, CHANNELS), f32),
            vmem((8 + BLOCK, 2 * STATE), f32),
            vmem((ROWS, CHANNELS), f32),
            vmem((ROWS, 2 * STATE), f32),
            vmem((ROWS, CHANNELS), f32),
            vmem((ROWS, CHANNELS), f32),
            vmem((CHUNKS, STATE, CHANNELS), bf16),
            vmem((8, BLOCK), f32),
            vmem((NCTX, 8, BLOCK), f32),
            vmem((NCTX, 16, 256), bf16),
            vmem((NCTX, 16, 256), bf16),
            vmem((NCTX, 16, 256), bf16),
            vmem((NCTX, 16, 256), bf16),
            vmem((NTP, 8, BLOCK), f32),
            dma((2,)), dma((NCTX,)), dma((NCTX,)), dma((NCTX,)), dma((NTP,)),
            dma((2,)), dma((NCTX,)), dma((NCTX,)), dma((NCTX,)), dma((NTP,)),
        ],
        compiler_params=pltpu.CompilerParams(
            collective_id=1, has_side_effects=True, vmem_limit_bytes=56 << 20
        ),
        cost_estimate=pl.CostEstimate(
            flops=2 * 10**9, bytes_accessed=6 << 20, transcendentals=3 * 10**6
        ),
        name="mixer",
    )(segments, *arrays)


def local(
    queries, key_rows, value_rows, segments, gate_input, state_proj, step_input, step_bias,
    decay_rate, skip_gain, conv_input, conv_state, norm_gain,
):
    qt = queries.reshape(CHUNKS, BLOCK, HEADS, HEAD_DIM).transpose(0, 3, 2, 1)
    qt = qt.reshape(CHUNKS, HEAD_DIM, HEADS * BLOCK)
    vt = value_rows.reshape(CHUNKS, BLOCK, HEAD_DIM).transpose(0, 2, 1)
    kv = jnp.concatenate([key_rows.reshape(ROWS, HEAD_DIM), vt.reshape(ROWS, HEAD_DIM)])
    attended = attention(segments, qt, kv)
    mixer_out = mixer(
        segments,
        attended,
        gate_input,
        state_proj.reshape(ROWS, 2 * STATE),
        step_input,
        step_input.T,
        step_bias[None, :],
        step_bias[:, None],
        decay_rate[None, :],
        decay_rate[:, None],
        jnp.repeat(skip_gain, SSM_DIM)[None, :],
        conv_input,
        conv_state.reshape(4, 2 * STATE),
        norm_gain[None, :],
    )
    return attended, mixer_out


def solution(mesh):
    placed = (
        P("ctx", "tp", None),
        P("ctx", "tp", None),
        P("ctx", "tp", None),
        P(),
        P("ctx", "tp"),
        P("ctx", None, "tp", None),
        P("ctx", "tp"),
        P("tp"),
        P("tp"),
        P("tp"),
        P(None, "tp"),
        P(None, None, "tp", None),
        P("tp"),
    )
    return jax.shard_map(
        local,
        mesh=mesh,
        in_specs=placed,
        out_specs=(P("ctx", "tp"), P("ctx", "tp")),
        check_vma=False,
    )
```

time: 680 us -> 142 us (0.21)
  the two profiles are of different devices: /device:TPU:230 before, /device:TPU:1 now
where the time goes in v1:
time: 142 us; the launch traced here: 141 us
  Pallas kernels  125 us (88%)
  local copies, waits for them, and re-layouts  13.8 us (10%)
  other arithmetic  1.63 us (1%)
    pallas_call x1, Pallas kernels, attention(): pl.pallas_call(attention_kernel, out_shape=jax.ShapeDtypeStruct((ROWS, CH...  83 us
    pallas_call x1, Pallas kernels, mixer(): pl.pallas_call(mixer_kernel, out_shape=jax.ShapeDtypeStruct((ROWS, CHANNE...  42.4 us
    unnamed x13, local copies, waits for them, and re-layouts  6.48 us

profile of v1, /device:TPU:1, one launch (start us, length us, event | category | flops | bytes accessed | tf_op | source)
XLA Modules:
  0.0 141.4 jit_solution(2616538603043910590)
XLA Ops:
  0.6 0.0 copy-start
  0.6 1.4 copy.25
  2.0 0.7 broadcast_in_dim.22
  2.7 0.7 broadcast_in_dim_reshape.3.skip_ref
  3.4 1.3 copy.19.rate_t_ref
  4.7 1.3 copy.18.bias_t_ref
  6.1 1.0 copy.16
  7.1 1.6 %pad_maximum_fusion.kv_ref = bf16[1024,128]{1,0:T(8,128)(2,1)} fusion(bf16[512,128]{1,0:T(8,128)(2,1)S(1)} %bitcast.28, bf16[512,128]{1,0:T(8,128)(2,1)} %bitcast.32), kind=kLoop, calls=%fused_computation.1 | loop fusion | flops 524288 | bytes 524288 | tf_op jit(solution)/shard_map/concatenate | solution.py:597
  8.7 0.0 copy-start.3
  8.7 1.7 %copy.24 = bf16[64,8,2,128]{3,1,2,0:T(8,128)(2,1)} copy(bf16[64,8,2,128]{3,2,1,0:T(2,128)(2,1)} %bitcast.29) | data formatting | bytes 524288
  10.4 0.0 copy-done.3
  10.4 0.8 copy.17.step_ref
  11.3 0.0 copy-done
  11.3 0.9 copy.15
  12.2 1.3 reshape.26.qt_ref
  13.5 83.0 %attention.1.att_ref = bf16[512,1024]{1,0:T(8,128)(2,1)} custom-call(s32[128]{0:T(128)} %seg_ref.3, bf16[4,128,1024]{2,1,0:T(8,128)(2,1)} %reshape.26.qt_ref, bf16[1024,128]{1,0:T(8,128)(2,1)} %pad_maximum_fusion.kv_ref), custom_call_target="tpu_custom_call" | custom-call | flops 20000000000 | bytes 4194304 | tf_op jit(solution)/shard_map/attention/pallas_call | solution.py:265
  96.5 0.0 copy-start.1
  96.5 42.4 %mixer.1 = bf16[512,1024]{1,0:T(8,128)(2,1)} custom-call(s32[128]{0:T(128)} %seg_ref.3, bf16[512,1024]{1,0:T(8,128)(2,1)} %attention.1.att_ref, bf16[512,1024]{1,0:T(8,128)(2,1)} %gate_ref.1, bf16[512,256]{1,0:T(8,128)(2,1)} %bitcast.30, f32[512,16]{1,0:T(8,128)} %copy.17.step_ref, f32[16,512]{1,0:T(8,128)} %bitcast.33, f32[1,16]{1,0:T(1,128)} %bitcast.37, ...), custom_call_target="tpu_custom_call" | custom-call | flops 2000000000 | bytes 6291456 | tf_op jit(solution)/shard_map/mixer/pallas_call | solution.py:554
  138.8 0.0 copy-done.1
  138.8 0.0 copy-start.2
  138.9 1.0 copy.28
  139.8 0.6 copy-done.2
  140.5 1.0 copy.29
Async XLA Ops:
  0.6 10.6 %copy-start = (bf16[512,8,128]{2,1,0:T(8,128)(2,1)S(1)}, bf16[512,8,128]{2,1,0:T(8,128)(2,1)}, u32[]{:S(2)}) copy-start(bf16[512,8,128]{2,1,0:T(8,128)(2,1)} %param.13) | copy-start | bytes 3145732
  8.7 1.7 %copy-start.3 = (f32[512,16]{0,1:T(8,128)S(1)}, f32[512,16]{0,1:T(8,128)}, u32[]{:S(2)}) copy-start(f32[512,16]{0,1:T(8,128)} %param.19) | copy-start | bytes 98308
  96.5 42.4 %copy-start.1 = (bf16[512,1024]{1,0:T(8,128)(2,1)S(1)}, bf16[512,1024]{1,0:T(8,128)(2,1)}, u32[]{:S(2)}) copy-start(bf16[512,1024]{1,0:T(8,128)(2,1)} %attention.1.att_ref) | copy-start | bytes 3145732
  138.8 1.6 %copy-start.2 = (bf16[512,1024]{1,0:T(8,128)(2,1)S(1)}, bf16[512,1024]{1,0:T(8,128)(2,1)}, u32[]{:S(2)}) copy-start(bf16[512,1024]{1,0:T(8,128)(2,1)} %mixer.1) | copy-start | bytes 3145732

commit v2 on v1

v2 whole, which is shorter than its diff:
```python
import functools
import math

import jax
import jax.numpy as jnp
from jax import lax
from jax.experimental import pallas as pl
from jax.experimental.pallas import tpu as pltpu
from jax.sharding import PartitionSpec as P

BLOCK = 128
NCTX = 32
NX = 4
NZ = 8
NTP = 8
ROWS = 512
HEADS = 8
HEAD_DIM = 128
SSM_HEADS = 16
SSM_DIM = 64
CHANNELS = 1024
STATE = 128
CHUNKS = ROWS // BLOCK
ALL_CHANNELS = 8192
NORM_EPS = 1e-05
EXP_SCALE = math.log2(math.e) / math.sqrt(HEAD_DIM)
HOPS = 6
FOLD_ORDER = (
    (1, 0), (2, 0), (0, 1), (0, 3), (0, 2), (1, 1), (3, 0), (1, 3), (1, 2),
    (2, 1), (4, 0), (2, 3), (2, 2), (3, 1), (3, 3), (3, 2), (4, 1), (4, 2),
)
STEPS = (
    (),
    (("z", 3), ("h", 0), ("h", 1)),
    (("x", 2),),
    (("z", 4),),
    (("h", 2), ("x", 3)),
    (("x", 4),),
    (("h", 3), ("h", 4)),
    (),
    (("x", 5), ("h", 5)),
)

f32 = jnp.float32
bf16 = jnp.bfloat16
HIGHEST = lax.Precision.HIGHEST
MESH_ID = pl.DeviceIdType.MESH


def dot(a, b, ca=1, cb=0, precision=None):
    return lax.dot_general(
        a, b, (((ca,), (cb,)), ((), ())), precision=precision, preferred_element_type=f32
    )


def remote(src, dst, send_sem, recv_sem, device):
    return pltpu.make_async_remote_copy(
        src_ref=src,
        dst_ref=dst,
        send_sem=send_sem,
        recv_sem=recv_sem,
        device_id=device,
        device_id_type=MESH_ID,
    )


def pick(table, n):
    value = jnp.int32(table[0])
    for i in range(1, len(table)):
        value = jnp.where(n >= i, jnp.int32(table[i]), value)
    return value


def silu(v):
    return v / (1.0 + jnp.exp(-v))


def softplus(v):
    return jnp.maximum(v, 0.0) + jnp.log1p(jnp.exp(-jnp.abs(v)))


def split(v):
    high = v.astype(bf16)
    return high, (v - high.astype(f32)).astype(bf16)


def spread(v, expand):
    high, low = split(v)
    return dot(high, expand) + dot(low, expand)


def chunk(c):
    return slice(c * BLOCK, (c + 1) * BLOCK)


def layer_kernel(
    seg_ref, q_ref, k_ref, v_ref, gate_ref, proj_ref, step_ref, bias_ref, rate_ref, skip_ref,
    tap_ref, tap_state_ref, gain_ref, att_ref, out_ref,
    wide, qt, kv, slots, m_s, l_s, acc_s,
    halo_a, halo_s, tail_a, tail_s, ext, ext_s, xs, cs, gs, mix_s, frag, heads_s, row_s,
    t_send, t_all, s_send, s_in, p_send, p_in, q_all,
    send_z, send_p, send_m, send_a, send_b, send_c,
    recv_z, recv_p, recv_m, recv_a, recv_b, recv_c,
    halo_sems, t_sems, s_sems, p_sems, q_sems,
    halo_recv, t_recv, s_recv, p_recv, q_recv,
):
    me = lax.axis_index("ctx")
    tp = lax.axis_index("tp")
    z, x = me // NX, me % NX
    up = {"ctx": lax.rem(z + 1, NZ) * NX + x}
    right = {"ctx": z * NX + lax.rem(x + 1, NX)}
    left = {"ctx": z * NX + lax.rem(x + NX - 1, NX)}

    barrier = pltpu.get_barrier_semaphore()

    def greet_ctx(o, c):
        pl.semaphore_signal(
            barrier, inc=1, device_id={"ctx": lax.rem(me + o, NCTX)}, device_id_type=MESH_ID
        )
        return c

    def greet_tp(o, c):
        pl.semaphore_signal(
            barrier, inc=1, device_id={"tp": lax.rem(tp + o, NTP)}, device_id_type=MESH_ID
        )
        return c

    lax.fori_loop(1, NCTX, greet_ctx, 0)
    lax.fori_loop(1, NTP, greet_tp, 0)

    half = ROWS
    kv[0:half] = k_ref[...]
    for c in range(CHUNKS):
        kv[half + c * BLOCK : half + (c + 1) * BLOCK] = (
            v_ref[chunk(c), :].astype(f32).T.astype(bf16)
        )
    tail_s[...] = proj_ref[2 * ROWS - 32 :, :]

    pl.semaphore_wait(barrier, NCTX - 1 + NTP - 1)

    def copy_z(k):
        return remote(
            kv if k == 0 else slots.at[k, 0], slots.at[k + 1, 0], send_z.at[k], recv_z.at[k + 1], up
        )

    def copy_p(k):
        return remote(
            kv if k == 0 else slots.at[k, 0], slots.at[k, 1], send_p.at[k], recv_p.at[k], right
        )

    def copy_m(k):
        return remote(
            kv if k == 0 else slots.at[k, 0], slots.at[k, 3], send_m.at[k], recv_m.at[k], left
        )

    def copy_a(k):
        rows = pl.ds(0, 2 * half if k == 0 else half)
        return remote(
            slots.at[k, 1, rows], slots.at[k, 2, rows], send_a.at[k], recv_a.at[k], right
        )

    def copy_b(k):
        rows = pl.ds(half, half)
        return remote(
            slots.at[k, 3, rows], slots.at[k, 2, rows], send_b.at[k], recv_b.at[k], left
        )

    def copy_c(k):
        return remote(
            slots.at[k - 1, 2], slots.at[k, 2], send_c.at[k], recv_c.at[k], up
        )

    def copy_d(k):
        return remote(
            slots.at[k - 1, 1], slots.at[k, 1], send_p.at[k], recv_p.at[k], up
        )

    top = HOPS - 1
    through_z = (2,)
    always = None
    moves = {("z", k): (copy_z, always, always) for k in range(top - 1)}
    for k in range(1, top):
        moves["p", k] = (copy_p, always, always)
        moves["m", k] = (copy_m, always, always)
        if k in through_z:
            moves["c", k] = (copy_c, always, always)
        else:
            moves["a", k] = (copy_a, always, always)
            moves["b", k] = (copy_b, always, always)
    moves["p", 0] = (copy_p, x < 3, x >= 1)
    moves["m", 0] = (copy_m, x == 0, x == 3)
    moves["a", 0] = (copy_a, (x == 1) | (x == 2), x >= 2)
    moves["d", top] = (copy_d, x == 0, x == 0)
    moves["c", top] = (copy_c, x <= 1, x <= 1)

    def act(kind, k, what):
        if (kind, k) not in moves:
            return
        make, sends, receives = moves[kind, k]
        condition = receives if what == "wait_recv" else sends

        def do():
            getattr(make(k), what)()

        if condition is None:
            do()
        else:
            pl.when(condition)(do)

    def z_step(k):
        if k > 0:
            act("z", k - 1, "wait_recv")
        for kind in ("z", "p", "m"):
            act(kind, k, "start")

    def x_step(k):
        act("p", k, "wait_recv")
        act("a", k, "start")
        act("m", k, "wait_recv")
        act("b", k, "start")
        act("d", k, "wait_recv")
        act("d", k + 1, "start")

    def h_step(k):
        for kind in ("a", "b", "c"):
            act(kind, k, "wait_recv")
        act("c", k + 1, "start")

    z_step(0)

    following = {"ctx": lax.rem(me + 1, NCTX)}
    send_proj = remote(tail_s, halo_s, halo_sems.at[1], halo_recv.at[1], following)
    send_proj.start()

    def t_copy(o, slot):
        return remote(
            t_send, t_all.at[slot], t_sems.at[o], t_recv.at[slot], {"ctx": lax.rem(me + o, NCTX)}
        )

    def s_copy(o, slot):
        to = lax.rem(me + o, NCTX)
        return remote(s_send.at[to], s_in.at[slot], s_sems.at[o], s_recv.at[slot], {"ctx": to})

    def p_copy(o, slot):
        to = lax.rem(me + o, NCTX)
        return remote(p_send.at[to], p_in.at[slot], p_sems.at[o], p_recv.at[slot], {"ctx": to})

    def q_copy(o, slot):
        return remote(
            q_all.at[tp], q_all.at[slot], q_sems.at[o], q_recv.at[slot],
            {"tp": lax.rem(tp + o, NTP)},
        )

    def start_all(copy, count, place):
        def one(o, c):
            copy(o, place).start()
            return c

        lax.fori_loop(1, count, one, 0)

    def recv_all(copy, count, place):
        def one(o, c):
            copy(o, lax.rem(place + o, count)).wait_recv()
            return c

        lax.fori_loop(1, count, one, 0)

    def sent_all(copy, count, place):
        def one(o, c):
            copy(o, place).wait_send()
            return c

        lax.fori_loop(1, count, one, 0)

    wide[...] = q_ref[...].astype(f32)
    for qb in range(CHUNKS):
        for h in range(HEADS):
            part = wide[pl.ds(qb * BLOCK * HEADS + h, BLOCK, stride=HEADS), :]
            qt[qb, :, h * BLOCK : (h + 1) * BLOCK] = part.T.astype(bf16)

    def scores(keys, qb, hp):
        return dot(keys, qt[qb, :, hp * 256 : (hp + 1) * 256])

    own_seg = [seg_ref[me * CHUNKS + c] for c in range(CHUNKS)]
    key_pos = lax.broadcasted_iota(jnp.int32, (BLOCK, 256), 0)
    query_pos = lax.broadcasted_iota(jnp.int32, (BLOCK, 256), 1) % BLOCK
    causal = key_pos <= query_pos
    tiles = [(qb, hp) for qb in range(CHUNKS) for hp in range(4)]

    def own_soft(qb, s):
        pens = [jnp.where(own_seg[b] == own_seg[qb], 0.0, 1e30).astype(f32) for b in range(qb)]
        last = jnp.where(causal, s[qb * BLOCK :], -1e30)
        m = jnp.max(last, axis=0, keepdims=True) * EXP_SCALE
        for b in range(qb):
            most = jnp.max(s[b * BLOCK : (b + 1) * BLOCK], axis=0, keepdims=True)
            m = jnp.maximum(m, most * EXP_SCALE - pens[b])
        total = jnp.zeros_like(m)
        parts = []
        for b in range(qb + 1):
            if b < qb:
                p = jnp.exp2(s[b * BLOCK : (b + 1) * BLOCK] * EXP_SCALE - (m + pens[b]))
            else:
                p = jnp.where(causal, jnp.exp2(last * EXP_SCALE - m), 0.0)
            total = total + jnp.sum(p, axis=0, keepdims=True)
            parts.append(p.astype(bf16))
        return m, total, jnp.concatenate(parts, axis=0)

    def values(block, count):
        return jnp.concatenate(
            [block[half + b * BLOCK : half + (b + 1) * BLOCK] for b in range(count)], axis=1
        )

    def own_fold(t, m, total, p):
        qb, hp = t
        i = qb * 4 + hp
        m_s[i] = m
        l_s[i] = total
        acc_s[i] = dot(values(kv, qb + 1), p)

    s_now = scores(kv[0:BLOCK], 0, 0)
    waiting = None
    for n, t in enumerate(tiles):
        s_next = None
        if n + 1 < len(tiles):
            qb, hp = tiles[n + 1]
            s_next = scores(kv[0 : (qb + 1) * BLOCK], qb, hp)
        done = own_soft(t[0], s_now)
        if waiting is not None:
            own_fold(waiting[0], *waiting[1])
        waiting = (t, done)
        s_now = s_next
    own_fold(waiting[0], *waiting[1])

    iota_r = lax.broadcasted_iota(jnp.int32, (BLOCK, BLOCK), 0)
    iota_c = lax.broadcasted_iota(jnp.int32, (BLOCK, BLOCK), 1)
    lower = iota_r >= iota_c
    tri = jnp.where(lower, 1.0, 0.0).astype(f32)
    expand = jnp.where(
        lax.broadcasted_iota(jnp.int32, (SSM_HEADS, CHANNELS), 1) // SSM_DIM
        == lax.broadcasted_iota(jnp.int32, (SSM_HEADS, CHANNELS), 0),
        1.0,
        0.0,
    ).astype(bf16)
    diagonal = lax.broadcasted_iota(jnp.int32, (SSM_HEADS, SSM_HEADS), 0) == (
        lax.broadcasted_iota(jnp.int32, (SSM_HEADS, SSM_HEADS), 1)
    )

    def as_column(row):
        square = jnp.broadcast_to(row, (SSM_HEADS, SSM_HEADS))
        return jnp.sum(jnp.where(diagonal, square, 0.0), axis=1, keepdims=True)

    bias = as_column(bias_ref[...])
    rate = as_column(rate_ref[...])
    keep = []
    for c in range(CHUNKS):
        at = me * CHUNKS + c
        same = (at > 0) & (seg_ref[at] == seg_ref[jnp.maximum(at - 1, 0)])
        keep.append(jnp.where(same, 1.0, 0.0).astype(f32))
    dt_t = [softplus(step_ref[:, chunk(c)] + bias) for c in range(CHUNKS)]
    cum_t = [dot(-dt_t[c] * rate, tri, 1, 1, precision=HIGHEST) for c in range(CHUNKS)]
    cum = [v.T for v in cum_t]
    last = [v[BLOCK - 1 : BLOCK, :] for v in cum]
    factor = [keep[c] * jnp.exp(last[c]) for c in range(CHUNKS)]
    prefix = [jnp.ones_like(last[0])]
    for c in range(CHUNKS):
        prefix.append(prefix[-1] * factor[c])
    t_send[...] = jnp.zeros_like(t_send)
    t_send[0:1, 0:SSM_HEADS] = prefix[CHUNKS]
    start_all(t_copy, NCTX, me)
    t_all[me] = t_send[...]
    for c in range(CHUNKS):
        begin = jnp.exp(cum[c]) * keep[c]
        heads_s[0, chunk(c), :] = jnp.exp(last[c] - cum[c]) * dt_t[c].T
        heads_s[1, chunk(c), :] = begin
        heads_s[2, chunk(c), :] = begin * prefix[c]
    rows = factor + [skip_ref[...]]
    rows = jnp.concatenate(rows + [jnp.zeros((8 - len(rows), SSM_HEADS), f32)], axis=0)
    row_s[...] = spread(rows, expand)

    z_step(1)

    send_proj.wait_recv()
    wide[0 : 2 * ROWS, :] = proj_ref[...].astype(f32)
    wide[2 * ROWS : 2 * ROWS + 32, :] = halo_s[...].astype(f32)
    for c in range(CHUNKS):
        for r in range(2):
            cols = slice(r * STATE, (r + 1) * STATE)
            first = 2 * ROWS + 16 if c == 0 else 2 * (c * BLOCK - 8)
            ext_s[0:8, cols] = wide[pl.ds(first + r, 8, stride=2), :] * keep[c]
            ext_s[8:, cols] = wide[pl.ds(2 * c * BLOCK + r, BLOCK, stride=2), :]
            conv = tap_state_ref[r : r + 1, :] * ext_s[8 : 8 + BLOCK, cols]
            for k in range(1, 4):
                tap = tap_state_ref[2 * k + r : 2 * k + r + 1, :]
                conv = conv + tap * ext_s[8 - k : 8 - k + BLOCK, cols]
            cs[chunk(c), cols] = silu(conv)
        meet = dot(cs[chunk(c), STATE:], cs[chunk(c), 0:STATE], 1, 1, precision=HIGHEST)
        for h in range(SSM_HEADS):
            gap = cum[c][:, h : h + 1] - cum_t[c][h : h + 1, :]
            mix = jnp.exp(jnp.where(lower, gap, 0.0)) * meet * dt_t[c][h : h + 1, :]
            mix_s[c, h // 2, :, (h % 2) * BLOCK : (h % 2 + 1) * BLOCK] = jnp.where(
                lower, mix, 0.0
            ).astype(bf16)
        gs[chunk(c), :] = silu(gate_ref[chunk(c), :].astype(f32))
        if c == CHUNKS - 2:
            x_step(0)
            x_step(1)
            z_step(2)

    def soft(i, s, pens):
        m = m_s[i]
        new = m
        for b, pen in enumerate(pens):
            most = jnp.max(s[b * BLOCK : (b + 1) * BLOCK], axis=0, keepdims=True)
            new = jnp.maximum(new, most * EXP_SCALE - pen)
        total = jnp.zeros_like(m)
        parts = []
        for b, pen in enumerate(pens):
            p = jnp.exp2(s[b * BLOCK : (b + 1) * BLOCK] * EXP_SCALE - (new + pen))
            total = total + jnp.sum(p, axis=0, keepdims=True)
            parts.append(p.astype(bf16))
        shrink = jnp.exp2(m - new)
        m_s[i] = new
        l_s[i] = l_s[i] * shrink + total
        return shrink, jnp.concatenate(parts, axis=0)

    by_name = {"z": z_step, "x": x_step, "h": h_step}

    def all_steps(steps):
        for name, k in steps:
            by_name[name](k)

    def fold_pair(n, carry):
        for at, steps in enumerate(STEPS):
            if steps:
                pl.when(n == at)(functools.partial(all_steps, steps))
        pens = [[] for _ in range(CHUNKS)]
        keys, vt = [], []
        for e in range(2):
            rank = pick([o[0] for o in FOLD_ORDER[e::2]], n)
            col = pick([o[1] for o in FOLD_ORDER[e::2]], n)
            source = me - (NX * rank + col)
            k = jnp.where(x >= col, rank, rank + 1)
            first = jnp.maximum(source, 0) * CHUNKS
            for b in range(CHUNKS):
                key_seg = seg_ref[first + b]
                for qb in range(CHUNKS):
                    allowed = (source >= 0) & (key_seg == own_seg[qb])
                    pens[qb].append(jnp.where(allowed, 0.0, 1e30).astype(f32))
                vt.append(slots[k, col, half + b * BLOCK : half + (b + 1) * BLOCK])
            keys.append(slots[k, col, 0:half])
        keys = jnp.concatenate(keys, axis=0)
        vt = jnp.concatenate(vt, axis=1)

        def fold(t, shrink, p):
            i = t[0] * 4 + t[1]
            acc_s[i] = acc_s[i] * shrink + dot(vt, p)

        s_now = scores(keys, 0, 0)
        waiting = None
        for n_tile, t in enumerate(tiles):
            s_next = scores(keys, *tiles[n_tile + 1]) if n_tile + 1 < len(tiles) else None
            done = soft(t[0] * 4 + t[1], s_now, pens[t[0]])
            if waiting is not None:
                fold(waiting[0], *waiting[1])
            waiting = (t, done)
            s_now = s_next
        fold(waiting[0], *waiting[1])
        return carry

    lax.fori_loop(0, len(STEPS), fold_pair, 0)

    send_att = remote(tail_a, halo_a, halo_sems.at[0], halo_recv.at[0], following)
    for qb, hp in reversed(tiles):
        i = qb * 4 + hp
        o = acc_s[i] / l_s[i]
        for j in range(2):
            c = (hp * 2 + j) * HEAD_DIM
            part = o[:, j * BLOCK : (j + 1) * BLOCK].T
            att_ref[chunk(qb), c : c + HEAD_DIM] = part.astype(bf16)
        if (qb, hp) == (CHUNKS - 1, 0):
            tail_a[...] = att_ref[ROWS - 16 :, :]
            send_att.start()

    for c in (1, 2, 3, 0):
        if c == 0:
            send_att.wait_recv()
            ext[0:8] = halo_a[...].astype(f32)[8:16] * keep[c]
        else:
            before = att_ref[c * BLOCK - 16 : c * BLOCK, :]
            ext[0:8] = before.astype(f32)[8:16] * keep[c]
        ext[8:] = att_ref[chunk(c), :].astype(f32)
        conv = tap_ref[0:1, :] * ext[8 : 8 + BLOCK]
        for k in range(1, 4):
            conv = conv + tap_ref[k : k + 1, :] * ext[8 - k : 8 - k + BLOCK]
        conv = silu(conv)
        xs[chunk(c), :] = conv
        scaled = (conv * spread(heads_s[0, chunk(c), :], expand)).astype(bf16)
        write_t = cs[chunk(c), 0:STATE].T.astype(bf16)
        frag[c] = dot(write_t, scaled)
    state = frag[0]
    for c in range(1, CHUNKS):
        state = state * row_s[c : c + 1, :] + frag[c]
    for ng in range(8):
        for cg in range(4):
            s_send[ng * 4 + cg] = state[
                ng * 16 : (ng + 1) * 16, cg * 256 : (cg + 1) * 256
            ].astype(bf16)
    start_all(s_copy, NCTX, me)
    s_in[me] = s_send[me]

    low_half = lax.broadcasted_iota(jnp.int32, (BLOCK, BLOCK), 1) < SSM_DIM

    def inside(c, state):
        conv = xs[chunk(c), :]
        out = conv * row_s[CHUNKS : CHUNKS + 1, :]
        if c > 0:
            read = cs[chunk(c), STATE:].astype(bf16)
            out = out + dot(read, state.astype(bf16)) * spread(heads_s[1, chunk(c), :], expand)
        parts = []
        for pair in range(SSM_HEADS // 2):
            both = conv[:, pair * BLOCK : (pair + 1) * BLOCK]
            stacked = jnp.concatenate(
                [jnp.where(low_half, both, 0.0), jnp.where(low_half, 0.0, both)], axis=0
            ).astype(bf16)
            parts.append(dot(mix_s[c, pair], stacked))
        xs[chunk(c), :] = out + jnp.concatenate(parts, axis=1)

    state = None
    for c in range(CHUNKS):
        inside(c, state)
        state = frag[c] if c == 0 else state * row_s[c : c + 1, :] + frag[c]

    recv_all(t_copy, NCTX, me)
    share = lax.rem(me, 4)
    expand_share = jnp.where(
        lax.broadcasted_iota(jnp.int32, (BLOCK, 256), 1) // SSM_DIM + share * 4
        == lax.broadcasted_iota(jnp.int32, (BLOCK, 256), 0),
        1.0,
        0.0,
    ).astype(bf16)
    decays = spread(t_all[:, 0, :], expand_share)
    recv_all(s_copy, NCTX, me)
    running = jnp.zeros((16, 256), f32)
    for d in range(NCTX):
        p_send[d] = running.astype(bf16)
        running = running * decays[d : d + 1, :] + s_in[d].astype(f32)
    start_all(p_copy, NCTX, me)
    p_in[me] = p_send[me]
    recv_all(p_copy, NCTX, me)
    incoming = jnp.concatenate(
        [
            jnp.concatenate([p_in[ng * 4 + cg] for cg in range(4)], axis=1)
            for ng in range(8)
        ],
        axis=0,
    )
    squares = []
    for c in range(CHUNKS):
        begin = spread(heads_s[2, chunk(c), :], expand)
        out = xs[chunk(c), :] + dot(cs[chunk(c), STATE:].astype(bf16), incoming) * begin
        gated = out * gs[chunk(c), :]
        gs[chunk(c), :] = gated
        sq = gated * gated
        folded = sq[:, 0:BLOCK]
        for i in range(1, CHANNELS // BLOCK):
            folded = folded + sq[:, i * BLOCK : (i + 1) * BLOCK]
        squares.append(jnp.sum(folded.T, axis=0, keepdims=True))
    squares.append(jnp.zeros((8 - CHUNKS, BLOCK), f32))
    q_all[tp] = jnp.concatenate(squares, axis=0)
    start_all(q_copy, NTP, tp)
    recv_all(q_copy, NTP, tp)
    total = q_all[0]
    for i in range(1, NTP):
        total = total + q_all[i]
    scale = lax.rsqrt(total * (1.0 / ALL_CHANNELS) + NORM_EPS)
    for c in range(CHUNKS):
        by_row = jnp.broadcast_to(scale[c : c + 1, :], (BLOCK, BLOCK)).T
        for i in range(CHANNELS // BLOCK):
            cols = slice(i * BLOCK, (i + 1) * BLOCK)
            out_ref[chunk(c), cols] = (gs[chunk(c), cols] * gain_ref[:, cols] * by_row).astype(bf16)

    for kind, k in moves:
        act(kind, k, "wait_send")
    send_att.wait_send()
    send_proj.wait_send()
    sent_all(t_copy, NCTX, me)
    sent_all(s_copy, NCTX, me)
    sent_all(p_copy, NCTX, me)
    sent_all(q_copy, NTP, tp)


def local(
    queries, key_rows, value_rows, segments, gate_input, state_proj, step_input, step_bias,
    decay_rate, skip_gain, conv_input, conv_state, norm_gain,
):
    dma = pltpu.SemaphoreType.DMA
    vmem = pltpu.VMEM
    arrays = (
        queries.reshape(ROWS * HEADS, HEAD_DIM),
        key_rows.reshape(ROWS, HEAD_DIM),
        value_rows.reshape(ROWS, HEAD_DIM),
        gate_input,
        state_proj.reshape(2 * ROWS, STATE),
        step_input.T,
        step_bias[None, :],
        decay_rate[None, :],
        skip_gain[None, :],
        conv_input,
        conv_state.reshape(8, STATE),
        norm_gain[None, :],
    )
    return pl.pallas_call(
        layer_kernel,
        out_shape=(jax.ShapeDtypeStruct((ROWS, CHANNELS), bf16),) * 2,
        in_specs=[pl.BlockSpec(memory_space=pltpu.SMEM)]
        + [pl.BlockSpec(memory_space=pltpu.VMEM)] * len(arrays),
        out_specs=(pl.BlockSpec(memory_space=pltpu.VMEM),) * 2,
        scratch_shapes=[
            vmem((ROWS * HEADS, HEAD_DIM), f32),
            vmem((CHUNKS, HEAD_DIM, HEADS * BLOCK), bf16),
            vmem((2 * ROWS, HEAD_DIM), bf16),
            vmem((HOPS, NX, 2 * ROWS, HEAD_DIM), bf16),
            vmem((16, 1, 256), f32),
            vmem((16, 1, 256), f32),
            vmem((16, HEAD_DIM, 256), f32),
            vmem((16, CHANNELS), bf16),
            vmem((32, STATE), bf16),
            vmem((16, CHANNELS), bf16),
            vmem((32, STATE), bf16),
            vmem((8 + BLOCK, CHANNELS), f32),
            vmem((8 + BLOCK, 2 * STATE), f32),
            vmem((ROWS, CHANNELS), f32),
            vmem((ROWS, 2 * STATE), f32),
            vmem((ROWS, CHANNELS), f32),
            vmem((CHUNKS, SSM_HEADS // 2, BLOCK, 2 * BLOCK), bf16),
            vmem((CHUNKS, STATE, CHANNELS), f32),
            vmem((3, ROWS, SSM_HEADS), f32),
            vmem((8, CHANNELS), f32),
            vmem((8, BLOCK), f32),
            vmem((NCTX, 8, BLOCK), f32),
            vmem((NCTX, 16, 256), bf16),
            vmem((NCTX, 16, 256), bf16),
            vmem((NCTX, 16, 256), bf16),
            vmem((NCTX, 16, 256), bf16),
            vmem((NTP, 8, BLOCK), f32),
        ]
        + [dma((HOPS,))] * 12
        + [dma((2,)), dma((NCTX,)), dma((NCTX,)), dma((NCTX,)), dma((NTP,))] * 2,
        compiler_params=pltpu.CompilerParams(
            collective_id=0, has_side_effects=True, vmem_limit_bytes=60 << 20
        ),
        cost_estimate=pl.CostEstimate(
            flops=22 * 10**9, bytes_accessed=8 << 20, transcendentals=43 * 10**6
        ),
        name="layer",
    )(segments, *arrays)


def solution(mesh):
    placed = (
        P("ctx", "tp", None),
        P("ctx", "tp", None),
        P("ctx", "tp", None),
        P(),
        P("ctx", "tp"),
        P("ctx", None, "tp", None),
        P("ctx", "tp"),
        P("tp"),
        P("tp"),
        P("tp"),
        P(None, "tp"),
        P(None, None, "tp", None),
        P("tp"),
    )
    return jax.shard_map(
        local,
        mesh=mesh,
        in_specs=placed,
        out_specs=(P("ctx", "tp"), P("ctx", "tp")),
        check_vma=False,
    )
```

time: 142 us -> 116 us (0.82)
  Pallas kernels: 125 us -> 112 us
  local copies, waits for them, and re-layouts: 13.8 us -> 3.32 us
  other arithmetic: 1.63 us -> 0 us
    pallas_call x2 -> x1, Pallas kernels: 125 us -> 112 us  [local(): pl.pallas_call(layer_kernel, out_shape=(jax.ShapeDtypeStruct((ROWS, CHANN...]
    broadcast_in_dim x3 -> x0, local copies, waits for them, and re-layouts: 3.37 us -> none  [the longest x1 1.32 us: local(): decay_rate[:, None]]
    reshape x3 -> x0, local copies, waits for them, and re-layouts: 3.23 us -> none  [the longest x1 1.27 us: local(): qt = qt.reshape(CHUNKS, HEAD_DIM, HEADS * BLOCK)]
    unnamed x13 -> x4, local copies, waits for them, and re-layouts: 6.48 us -> 3.32 us
    concatenate x1 -> x0, other arithmetic: 1.63 us -> none  [local(): jnp.concatenate([key_rows.reshape(ROWS, HEAD_DIM), vt.reshape(ROWS, HEAD_...]
where the time goes in v2:
time: 116 us
  Pallas kernels  112 us (97%)
  local copies, waits for them, and re-layouts  3.32 us (3%)
    pallas_call x1, Pallas kernels, local(): pl.pallas_call(layer_kernel, out_shape=(jax.ShapeDtypeStruct((ROWS, CHANN...  112 us
    unnamed x4, local copies, waits for them, and re-layouts  3.32 us

profile of v2, /device:TPU:1, one launch (start us, length us, event | category | flops | bytes accessed | tf_op | source)
XLA Modules:
  0.0 115.9 jit_solution(11941005520522983798)
XLA Ops:
  0.6 111.9 %layer.1 = (bf16[512,1024]{1,0:T(8,128)(2,1)}, bf16[512,1024]{1,0:T(8,128)(2,1)}) custom-call(s32[128]{0:T(128)} %seg_ref.1, bf16[4096,128]{1,0:T(8,128)(2,1)} %bitcast.10, bf16[512,128]{1,0:T(8,128)(2,1)} %bitcast.12, bf16[512,128]{1,0:T(8,128)(2,1)} %bitcast.13, bf16[512,1024]{1,0:T(8,128)(2,1)} %gate_ref.1, bf16[1024,128]{1,0:T(8,128)(2,1)} %bitcast.11, ...), custom_call_target="tpu_custom_call" | custom-call | flops 22000001024 | bytes 8388608 | tf_op jit(solution)/shard_map/layer/pallas_call | solution.py:612
  112.5 0.0 copy-start
  112.5 2.4 %copy.17 = bf16[512,1024]{1,0:T(8,128)(2,1)} copy(bf16[512,1024]{1,0:T(8,128)(2,1)} %get-tuple-element.4) | data formatting | bytes 2097152
  114.9 0.0 copy-done
  114.9 1.0 copy.18
Async XLA Ops:
  112.5 2.4 %copy-start = (bf16[512,1024]{1,0:T(8,128)(2,1)S(1)}, bf16[512,1024]{1,0:T(8,128)(2,1)}, u32[]{:S(2)}) copy-start(bf16[512,1024]{1,0:T(8,128)(2,1)} %get-tuple-element.5) | copy-start | bytes 3145732

commit v3 on v2

--- a/solution.py
+++ b/solution.py
@@ -234,43 +234,45 @@
 
     def t_copy(o, slot):
         return remote(
-            t_send, t_all.at[slot], t_sems.at[o], t_recv.at[slot], {"ctx": lax.rem(me + o, NCTX)}
+            t_send, t_all.at[slot], t_sems, t_recv, {"ctx": lax.rem(me + o, NCTX)}
         )
 
     def s_copy(o, slot):
         to = lax.rem(me + o, NCTX)
-        return remote(s_send.at[to], s_in.at[slot], s_sems.at[o], s_recv.at[slot], {"ctx": to})
+        return remote(s_send.at[to], s_in.at[slot], s_sems, s_recv, {"ctx": to})
 
     def p_copy(o, slot):
         to = lax.rem(me + o, NCTX)
-        return remote(p_send.at[to], p_in.at[slot], p_sems.at[o], p_recv.at[slot], {"ctx": to})
+        return remote(p_send.at[to], p_in.at[slot], p_sems, p_recv, {"ctx": to})
 
     def q_copy(o, slot):
         return remote(
-            q_all.at[tp], q_all.at[slot], q_sems.at[o], q_recv.at[slot],
-            {"tp": lax.rem(tp + o, NTP)},
-        )
+            q_all.at[tp], q_all.at[slot], q_sems, q_recv, {"tp": lax.rem(tp + o, NTP)}
+        )
+
+    def everything(buffer, sems, recv, count):
+        part = buffer.at[pl.ds(0, count - 1)]
+        return remote(part, part, sems, recv, following)
+
+    exchanged = {
+        t_copy: everything(t_all, t_sems, t_recv, NCTX),
+        s_copy: everything(s_in, s_sems, s_recv, NCTX),
+        p_copy: everything(p_in, p_sems, p_recv, NCTX),
+        q_copy: everything(q_all, q_sems, q_recv, NTP),
+    }
 
     def start_all(copy, count, place):
         def one(o, c):
             copy(o, place).start()
             return c
 
-        lax.fori_loop(1, count, one, 0)
+        lax.fori_loop(1, count, one, 0, unroll=True)
 
     def recv_all(copy, count, place):
-        def one(o, c):
-            copy(o, lax.rem(place + o, count)).wait_recv()
-            return c
-
-        lax.fori_loop(1, count, one, 0)
+        exchanged[copy].wait_recv()
 
     def sent_all(copy, count, place):
-        def one(o, c):
-            copy(o, place).wait_send()
-            return c
-
-        lax.fori_loop(1, count, one, 0)
+        exchanged[copy].wait_send()
 
     wide[...] = q_ref[...].astype(f32)
     for qb in range(CHUNKS):
@@ -376,8 +378,6 @@
     rows = factor + [skip_ref[...]]
     rows = jnp.concatenate(rows + [jnp.zeros((8 - len(rows), SSM_HEADS), f32)], axis=0)
     row_s[...] = spread(rows, expand)
-
-    z_step(1)
 
     send_proj.wait_recv()
     wide[0 : 2 * ROWS, :] = proj_ref[...].astype(f32)
@@ -401,6 +401,8 @@
                 lower, mix, 0.0
             ).astype(bf16)
         gs[chunk(c), :] = silu(gate_ref[chunk(c), :].astype(f32))
+        if c == 0:
+            z_step(1)
         if c == CHUNKS - 2:
             x_step(0)
             x_step(1)
@@ -645,7 +647,7 @@
             vmem((NTP, 8, BLOCK), f32),
         ]
         + [dma((HOPS,))] * 12
-        + [dma((2,)), dma((NCTX,)), dma((NCTX,)), dma((NCTX,)), dma((NTP,))] * 2,
+        + [dma((2,)), dma(()), dma(()), dma(()), dma(())] * 2,
         compiler_params=pltpu.CompilerParams(
             collective_id=0, has_side_effects=True, vmem_limit_bytes=60 << 20
         ),

time: 116 us -> 112 us (0.966)
  Pallas kernels: 112 us -> 108 us
    pallas_call x1, Pallas kernels: 112 us -> 108 us  [local(): pl.pallas_call(layer_kernel, out_shape=(jax.ShapeDtypeStruct((ROWS, CHANN...]
where the time goes in v3:
time: 112 us
  Pallas kernels  108 us (96%)
  local copies, waits for them, and re-layouts  3.32 us (3%)
    pallas_call x1, Pallas kernels, local(): pl.pallas_call(layer_kernel, out_shape=(jax.ShapeDtypeStruct((ROWS, CHANN...  108 us
    unnamed x4, local copies, waits for them, and re-layouts  3.32 us

profile of v3, /device:TPU:1, one launch (start us, length us, event | category | flops | bytes accessed | tf_op | source)
XLA Modules:
  0.0 112.2 jit_solution(4714146031857387003)
XLA Ops:
  0.6 108.2 %layer.1 = (bf16[512,1024]{1,0:T(8,128)(2,1)}, bf16[512,1024]{1,0:T(8,128)(2,1)}) custom-call(s32[128]{0:T(128)} %seg_ref.1, bf16[4096,128]{1,0:T(8,128)(2,1)} %bitcast.10, bf16[512,128]{1,0:T(8,128)(2,1)} %bitcast.12, bf16[512,128]{1,0:T(8,128)(2,1)} %bitcast.13, bf16[512,1024]{1,0:T(8,128)(2,1)} %gate_ref.1, bf16[1024,128]{1,0:T(8,128)(2,1)} %bitcast.11, ...), custom_call_target="tpu_custom_call" | custom-call | flops 22000001024 | bytes 8388608 | tf_op jit(solution)/shard_map/layer/pallas_call | solution.py:614
  108.8 0.0 copy-start
  108.8 2.4 %copy.17 = bf16[512,1024]{1,0:T(8,128)(2,1)} copy(bf16[512,1024]{1,0:T(8,128)(2,1)} %get-tuple-element.4) | data formatting | bytes 2097152
  111.2 0.0 copy-done
  111.2 1.0 copy.18
Async XLA Ops:
  108.8 2.4 %copy-start = (bf16[512,1024]{1,0:T(8,128)(2,1)S(1)}, bf16[512,1024]{1,0:T(8,128)(2,1)}, u32[]{:S(2)}) copy-start(bf16[512,1024]{1,0:T(8,128)(2,1)} %get-tuple-element.5) | copy-start | bytes 3145732

commit v4 on v3

--- a/solution.py
+++ b/solution.py
@@ -31,8 +31,8 @@
 )
 STEPS = (
     (),
-    (("z", 3), ("h", 0), ("h", 1)),
-    (("x", 2),),
+    (("z", 3),),
+    (("x", 2), ("h", 0), ("h", 1)),
     (("z", 4),),
     (("h", 2), ("x", 3)),
     (("x", 4),),
@@ -197,7 +197,15 @@
         if (kind, k) not in moves:
             return
         make, sends, receives = moves[kind, k]
-        condition = receives if what == "wait_recv" else sends
+        row = k + 1 if kind == "z" else k
+        if what == "wait_recv":
+            condition, inside = receives, z >= row
+        else:
+            condition = sends
+            inside = z >= k if kind in "pmab" else z + 1 >= row
+            if kind in "zcd":
+                inside = inside & (z < NZ - 1)
+        condition = inside if condition is None else condition & inside
 
         def do():
             getattr(make(k), what)()
@@ -225,6 +233,13 @@
         for kind in ("a", "b", "c"):
             act(kind, k, "wait_recv")
         act("c", k + 1, "start")
+
+    for k in range(1, HOPS):
+
+        def clear(k=k):
+            slots[k] = jnp.zeros(slots.shape[1:], bf16)
+
+        pl.when(z < k)(clear)
 
     z_step(0)
 
@@ -527,10 +542,11 @@
             parts.append(dot(mix_s[c, pair], stacked))
         xs[chunk(c), :] = out + jnp.concatenate(parts, axis=1)
 
-    state = None
-    for c in range(CHUNKS):
+    state = frag[0]
+    inside(0, None)
+    for c in range(1, 2):
         inside(c, state)
-        state = frag[c] if c == 0 else state * row_s[c : c + 1, :] + frag[c]
+        state = state * row_s[c : c + 1, :] + frag[c]
 
     recv_all(t_copy, NCTX, me)
     share = lax.rem(me, 4)
@@ -548,6 +564,9 @@
         running = running * decays[d : d + 1, :] + s_in[d].astype(f32)
     start_all(p_copy, NCTX, me)
     p_in[me] = p_send[me]
+    for c in range(2, CHUNKS):
+        inside(c, state)
+        state = state * row_s[c : c + 1, :] + frag[c]
     recv_all(p_copy, NCTX, me)
     incoming = jnp.concatenate(
         [

time: 112 us -> 111 us (level)
  no operation moved by 1% of the time
where the time goes in v4:
time: 111 us
  Pallas kernels  107 us (96%)
  local copies, waits for them, and re-layouts  3.32 us (3%)
    pallas_call x1, Pallas kernels, local(): pl.pallas_call(layer_kernel, out_shape=(jax.ShapeDtypeStruct((ROWS, CHANN...  107 us
    unnamed x4, local copies, waits for them, and re-layouts  3.32 us

profile of v4, /device:TPU:1, one launch (start us, length us, event | category | flops | bytes accessed | tf_op | source)
XLA Modules:
  0.0 111.2 jit_solution(13288561756521850302)
XLA Ops:
  0.6 107.2 %layer.1 = (bf16[512,1024]{1,0:T(8,128)(2,1)}, bf16[512,1024]{1,0:T(8,128)(2,1)}) custom-call(s32[128]{0:T(128)} %seg_ref.1, bf16[4096,128]{1,0:T(8,128)(2,1)} %bitcast.10, bf16[512,128]{1,0:T(8,128)(2,1)} %bitcast.12, bf16[512,128]{1,0:T(8,128)(2,1)} %bitcast.13, bf16[512,1024]{1,0:T(8,128)(2,1)} %gate_ref.1, bf16[1024,128]{1,0:T(8,128)(2,1)} %bitcast.11, ...), custom_call_target="tpu_custom_call" | custom-call | flops 22000001024 | bytes 8388608 | tf_op jit(solution)/shard_map/layer/pallas_call | solution.py:633
  107.9 0.0 copy-start
  107.9 2.4 %copy.17 = bf16[512,1024]{1,0:T(8,128)(2,1)} copy(bf16[512,1024]{1,0:T(8,128)(2,1)} %get-tuple-element.4) | data formatting | bytes 2097152
  110.3 0.0 copy-done
  110.3 1.0 copy.18
Async XLA Ops:
  107.9 2.4 %copy-start = (bf16[512,1024]{1,0:T(8,128)(2,1)S(1)}, bf16[512,1024]{1,0:T(8,128)(2,1)}, u32[]{:S(2)}) copy-start(bf16[512,1024]{1,0:T(8,128)(2,1)} %get-tuple-element.5) | copy-start | bytes 3145732
